TPU v7x, 32 devices: a whole 2x2x4 slice. The times are simulated.
32 devices in a mesh: feat: 4 (over y, core), dom: 8 (over z, x).
Axes of the slice: x: 2, y: 2, z: 4, core: 2. Of those that a mesh axis runs over, the one named last changes fastest.
Arguments:
- features: bfloat16 [4, 1024, 4096], P(None, 'dom', 'feat'), may hold values from -6 to 6
- w_one: bfloat16 [4096, 1024], P('feat'), may hold values from -0.09375 to 0.09375
- w_two: bfloat16 [1024, 512], replicated, may hold values from -0.25 to 0.25
- neighbor: int32 [4, 1024, 10], P('feat', 'dom'), may hold values from 0 to 191
- degree: int32 [4, 1024], P('feat', 'dom'), may hold values from 1 to 10
- send_rows: int32 [4, 64, 8], P('feat', 'dom'), may hold values from 0 to 127
- grad_out: bfloat16 [4, 1024, 512], P('feat', 'dom'), may hold values from -6 to 6
Outputs:
- out_two: bfloat16 [4, 1024, 512], P('feat', 'dom')
- grad_one: float32 [4096, 1024], P('feat')
- grad_two: float32 [1024, 512], replicated
All inputs are finite; a program needn't handle non-finite values.
Results may differ from a plain program's by a relative error of at most 0.015.
Values may be sent and summed in bfloat16 or wider, within the bound.
A program may use at most 64 MiB of HBM per device.

v0:
```python
import math

import jax
import jax.numpy as jnp
from jax import lax
from jax.sharding import PartitionSpec as P


def trade(buffer):
    return lax.all_to_all(buffer, "dom", split_axis=0, concat_axis=0, tiled=True)


def on_device(features, w_one, w_two, neighbor, degree, send_rows, grad_out):
    groups, nodes, cols = features.shape
    width = w_two.shape[1]
    nbrs = neighbor[0]
    degs = degree[0]
    sends = send_rows[0]
    parts = lax.axis_size("dom")
    fan = nbrs.shape[1]
    slots = jnp.arange(fan, dtype=jnp.int32)
    weight = (slots[None, :] < degs[:, None]).astype(jnp.float32) / degs[:, None].astype(
        jnp.float32
    )
    flat = features.reshape(groups * nodes, cols)

    def spread(values):
        boxes = values[sends]
        recv = trade(boxes)
        table = jnp.concatenate([values, recv.reshape(-1, values.shape[1])], axis=0)
        gathered = table[nbrs]
        return jnp.sum(gathered.astype(jnp.float32) * weight[..., None], axis=1)

    def gather_back(grads):
        span = grads.shape[1]
        terms = (weight[..., None] * grads[:, None, :]).reshape(-1, span)
        table = jnp.zeros((nodes + sends.size, span), jnp.float32).at[nbrs.reshape(-1)].add(terms)
        local = table[:nodes]
        outgoing = table[nodes:].astype(jnp.bfloat16).reshape(parts, sends.shape[1], span)
        returned = trade(outgoing)
        home = (
            jnp.zeros((nodes, span), jnp.float32)
            .at[sends.reshape(-1)]
            .add(returned.reshape(-1, span).astype(jnp.float32))
        )
        return local + home

    rows = flat
    proj = lax.psum_scatter(
        jnp.dot(rows, w_one, preferred_element_type=jnp.float32),
        "feat",
        scatter_dimension=0,
        tiled=True,
    )
    p_self = proj[:, :width]
    p_near = proj[:, width:].astype(jnp.bfloat16)
    pre = p_self + spread(p_near)
    hidden = (pre * jax.nn.sigmoid(pre)).astype(jnp.bfloat16)
    agg = spread(hidden).astype(jnp.bfloat16)
    joined = jnp.concatenate([hidden, agg], axis=-1)
    out = jnp.dot(joined, w_two, preferred_element_type=jnp.float32).astype(jnp.bfloat16)
    grads = grad_out[0]
    two_sum = lax.dot_general(
        joined, grads, (((0,), (0,)), ((), ())), preferred_element_type=jnp.float32
    )
    dcat = lax.dot_general(
        grads, w_two, (((1,), (1,)), ((), ())), preferred_element_type=jnp.float32
    )
    d_hidden = dcat[:, :width] + gather_back(dcat[:, width:])
    sig = jax.nn.sigmoid(pre)
    d_pre = d_hidden * sig * (1.0 + pre * (1.0 - sig))
    d_near = gather_back(d_pre)
    d_proj = jnp.concatenate([d_pre, d_near], axis=-1).astype(jnp.bfloat16)
    rows = flat
    one_sum = lax.dot_general(
        rows,
        lax.all_gather(d_proj, "feat", axis=0, tiled=True),
        (((0,), (0,)), ((), ())),
        preferred_element_type=jnp.float32,
    )
    one_sum = lax.psum(one_sum.astype(jnp.bfloat16), "dom").astype(jnp.float32)
    two_sum = lax.psum(two_sum, ("feat", "dom"))
    scale = 1.0 / math.sqrt(groups * nodes * parts)
    return (out[None], one_sum * scale, two_sum * scale)


def solution(mesh):
    in_specs = (
        P(None, "dom", "feat"),
        P("feat", None),
        P(),
        P("feat", "dom", None),
        P("feat", "dom"),
        P("feat", "dom", None),
        P("feat", "dom", None),
    )
    out_specs = (P("feat", "dom", None), P("feat", None), P())
    return jax.shard_map(
        on_device, mesh=mesh, in_specs=in_specs, out_specs=out_specs, check_vma=False
    )
```

profile of v0, /device:TPU:0, one launch (start us, length us, event | category | flops | bytes accessed | tf_op | source)
XLA Modules:
  0.0 390.2 jit_solution(8050504698502090572)
XLA Ops:
  8.8 3.8 fusion.26
  17.7 4.7 %mul.74 = f32[1280,512]{1,0:T(8,128)} reshape(f32[128,10,512]{2,1,0:T(8,128)} %mul.73) | data formatting | bytes 5242880 | tf_op jit(solution)/shard_map/mul | solution.py:36
  22.6 13.7 %scatter_custom_fusion = f32[192,512]{1,0:T(8,128)} fusion(s32[1280]{0:T(1024)S(1)} %fusion.21, f32[1280,512]{1,0:T(8,128)} %mul.74, f32[1280]{0:T(1024)S(1)} %div.23, f32[]{:T(128)} %constant.9.clone.1), kind=kCustom, calls=%fused_computation.13 | custom fusion | flops 1310720 | bytes 3022852 | tf_op jit(solution)/shard_map/scatter-add | solution.py:37
  37.9 7.0 %all-to-all-start.2 = ((bf16[8,8,512]{2,1,0:T(8,128)(2,1)}), bf16[8,8,512]{2,1,0:T(8,128)(2,1)S(1)}, u32[]{:S(2)}, u32[]{:S(2)}) async-start(bf16[8,8,512]{2,1,0:T(8,128)(2,1)} %fusion.17), calls=%async_computation.3 | async-start | bytes 131072 | tf_op jit(solution)/shard_map/all_to_all | solution.py:10
  51.8 4.0 %all-to-all-start = ((bf16[8,8,512]{2,1,0:T(8,128)(2,1)}), bf16[8,8,512]{2,1,0:T(8,128)(2,1)S(1)}, u32[]{:S(2)}, u32[]{:S(2)}) async-start(bf16[8,8,512]{2,1,0:T(8,128)(2,1)} %bitcast.2), calls=%async_computation.1 | async-start | bytes 131072 | tf_op jit(solution)/shard_map/all_to_all | solution.py:10
  58.5 2.7 scatter_custom_fusion.1
  64.2 4.7 %gather_fusion.1 = bf16[1280,512]{1,0:T(8,128)(2,1)} fusion(bf16[192,512]{1,0:T(8,128)(2,1)S(1)} %pad_maximum_fusion.2, s32[2048]{0:T(1024)S(1)} %pad_clamp_fusion), kind=kCustom, calls=%fused_computation.1 | custom fusion | bytes 2626560 | tf_op jit(solution)/shard_map/gather | solution.py:31
  68.9 3.8 reshape.277
  72.7 3.3 multiply_reduce_fusion.1
  78.7 4.5 %mul.80 = f32[1280,512]{1,0:T(8,128)} reshape(f32[128,10,512]{2,1,0:T(8,128)} %mul.79) | data formatting | bytes 5242880 | tf_op jit(solution)/shard_map/mul | solution.py:36
  83.2 13.6 %scatter_custom_fusion.2 = f32[192,512]{1,0:T(8,128)} fusion(s32[1280]{0:T(1024)} %copy-done.11, f32[1280,512]{1,0:T(8,128)} %mul.80, f32[1280]{0:T(1024)S(1)} %div.23, f32[]{:T(128)} %constant.9.clone.1), kind=kCustom, calls=%fused_computation.11 | custom fusion | flops 1310720 | bytes 3020288 | tf_op jit(solution)/shard_map/scatter-add | solution.py:37
  98.3 4.5 %all-to-all-start.3 = ((bf16[8,8,512]{2,1,0:T(8,128)(2,1)}), bf16[8,8,512]{2,1,0:T(8,128)(2,1)S(1)}, u32[]{:S(2)}, u32[]{:S(2)}) async-start(bf16[8,8,512]{2,1,0:T(8,128)(2,1)} %fusion.18), calls=%async_computation.4 | async-start | bytes 131072 | tf_op jit(solution)/shard_map/all_to_all | solution.py:10
  104.6 5.2 %all-to-all-done.3 = bf16[8,8,512]{2,1,0:T(8,128)(2,1)S(1)} async-done(((bf16[8,8,512]{2,1,0:T(8,128)(2,1)}), bf16[8,8,512]{2,1,0:T(8,128)(2,1)S(1)}, u32[]{:S(2)}, u32[]{:S(2)}) %all-to-all-start.3) | async-done | bytes 65568 | tf_op jit(solution)/shard_map/all_to_all | solution.py:10
  109.7 2.7 scatter_custom_fusion.3
  115.0 9.3 %all_to_all.20 = bf16[8,8,512]{2,1,0:T(8,128)(2,1)S(1)} all-to-all(bf16[8,8,512]{2,1,0:T(8,128)(2,1)S(1)} %bitcast.48), channel_id=1, replica_groups=mesh['feat'=4,'dom'=8] {'dom'}, dimensions={0} | all-to-all | bytes 131072 | tf_op jit(solution)/shard_map/all_to_all | solution.py:10
  124.3 4.7 %gather_fusion.3 = bf16[1280,512]{1,0:T(8,128)(2,1)} fusion(bf16[192,512]{1,0:T(8,128)(2,1)S(1)} %pad_maximum_fusion.3, s32[2048]{0:T(1024)S(1)} %pad_clamp_fusion), kind=kCustom, calls=%fused_computation.3 | custom fusion | bytes 2626560 | tf_op jit(solution)/shard_map/gather | solution.py:31
  129.1 3.8 reshape.278
  132.9 3.2 multiply_reduce_fusion
  138.2 4.2 %convert_bitcast_fusion = bf16[1024,1024]{0,1:T(8,128)(2,1)} fusion(bf16[512,1024]{1,0:T(8,128)(2,1)} %all-gather.2.cloned.1.call-done, bf16[512,1024]{1,0:T(8,128)(2,1)} %bitcast.53), kind=kOutput, calls=%fused_computation.15 | convolution fusion | flops 1074790400 | bytes 4194304 | tf_op jit(solution)/shard_map/dot_general | solution.py:75
  143.4 126.1 %all-reduce.5.cloned.1.call-done = f32[1024,512]{1,0:T(8,128)} async-done(((f32[1024,512]{1,0:T(8,128)}), f32[1024,512]{1,0:T(8,128)}) %all-reduce.5.cloned.1.call-update) | async-done | bytes 2097168 | tf_op jit(solution)/shard_map/psum | solution.py:82
  269.4 3.1 broadcast_multiply_fusion
  272.6 101.7 %all-reduce.3.cloned.1.call-done = bf16[1024,1024]{0,1:T(8,128)(2,1)} async-done(((bf16[1024,1024]{0,1:T(8,128)(2,1)}), bf16[1024,1024]{0,1:T(8,128)(2,1)}) %all-reduce.3.cloned.1.call-update) | async-done | bytes 2097168 | tf_op jit(solution)/shard_map/psum | solution.py:81
  374.2 4.1 %convert_multiply_fusion = f32[1024,1024]{0,1:T(8,128)} fusion(bf16[1024,1024]{0,1:T(8,128)(2,1)} %all-reduce.3.cloned.1.call-done), kind=kLoop, calls=%fused_computation.8 | loop fusion | flops 2097152 | bytes 6291456 | tf_op jit(solution)/shard_map/mul | solution.py:84
  378.4 5.3 %copy.13 = f32[1024,1024]{1,0:T(8,128)} copy(f32[1024,1024]{0,1:T(8,128)} %convert_multiply_fusion) | data formatting | bytes 8388608
  (71 shorter events, 32.6 us)
Async XLA Ops:
  7.2 1.6 copy-start
  7.2 40.3 %reduce-scatter.2.cloned.1.call-start = ((), (), s32[]{:S(2)}) async-start(), calls=%async_computation.5 | async-start | bytes 2621440 | tf_op jit(solution)/shard_map/reduce_scatter | solution.py:49
  8.8 3.9 copy-start.9
  8.8 4.1 %copy-start.4 = (bf16[1,128,512]{2,1,0:T(8,128)(2,1)S(1)}, bf16[1,128,512]{2,1,0:T(8,128)(2,1)}, u32[]{:S(2)}) copy-start(bf16[1,128,512]{2,1,0:T(8,128)(2,1)} %param.13) | copy-start | bytes 393220
  12.6 1.2 copy-start.1
  14.3 0.8 copy-start.2
  17.7 4.7 %copy-start.12 = (s32[1,128]{1,0:T(1,128)S(1)}, s32[1,128]{1,0:T(1,128)}, u32[]{:S(2)}) copy-start(s32[1,128]{1,0:T(1,128)} %param.11) | copy-start | bytes 1540
  22.3 24.9 %copy-start.10 = (s32[1,8,8]{2,1,0:T(8,128)S(1)}, s32[1,8,8]{2,1,0:T(8,128)}, u32[]{:S(2)}) copy-start(s32[1,8,8]{2,1,0:T(8,128)} %param.12) | copy-start | bytes 772
  22.6 24.8 %copy-start.11 = (s32[1280]{0:T(1024)}, s32[1280]{0:T(1024)S(1)}, u32[]{:S(2)}) copy-start(s32[1280]{0:T(1024)S(1)} %fusion.21) | copy-start | bytes 15364
  37.9 13.9 %all-to-all-start.2 = ((bf16[8,8,512]{2,1,0:T(8,128)(2,1)}), bf16[8,8,512]{2,1,0:T(8,128)(2,1)S(1)}, u32[]{:S(2)}, u32[]{:S(2)}) async-start(bf16[8,8,512]{2,1,0:T(8,128)(2,1)} %fusion.17), calls=%async_computation.3 | async-start | bytes 131072 | tf_op jit(solution)/shard_map/all_to_all | solution.py:10
  47.4 9.7 %copy-start.8 = (s32[1024]{0:T(1024)}, s32[1024]{0:T(1024)S(1)}, u32[]{:S(2)}) copy-start(s32[1024]{0:T(1024)S(1)} %pad_clamp_fusion.1) | copy-start | bytes 12292
  51.8 10.9 %all-to-all-start = ((bf16[8,8,512]{2,1,0:T(8,128)(2,1)}), bf16[8,8,512]{2,1,0:T(8,128)(2,1)S(1)}, u32[]{:S(2)}, u32[]{:S(2)}) async-start(bf16[8,8,512]{2,1,0:T(8,128)(2,1)} %bitcast.2), calls=%async_computation.1 | async-start | bytes 131072 | tf_op jit(solution)/shard_map/all_to_all | solution.py:10
  62.7 0.6 copy-start.7
  72.7 3.3 copy-start.3
  72.7 3.3 copy-start.6
  98.3 11.4 %all-to-all-start.3 = ((bf16[8,8,512]{2,1,0:T(8,128)(2,1)}), bf16[8,8,512]{2,1,0:T(8,128)(2,1)S(1)}, u32[]{:S(2)}, u32[]{:S(2)}) async-start(bf16[8,8,512]{2,1,0:T(8,128)(2,1)} %fusion.18), calls=%async_computation.4 | async-start | bytes 131072 | tf_op jit(solution)/shard_map/all_to_all | solution.py:10
  102.8 35.4 %all-gather.2.cloned.1.call-start = ((), (), s32[]{:S(2)}) async-start(), calls=%async_computation.6 | async-start | bytes 1310720 | tf_op jit(solution)/shard_map/all_gather | solution.py:77
  114.2 155.3 %all-reduce.5.cloned.1.call-start = ((), (), s32[]{:S(2)}) async-start(), calls=%async_computation.8 | async-start | bytes 4194304 | tf_op jit(solution)/shard_map/psum | solution.py:82
  132.9 3.2 copy-start.5
  137.9 236.3 %all-reduce.3.cloned.1.call-start = ((), (), s32[]{:S(2)}) async-start(), calls=%async_computation.7 | async-start | bytes 4194304 | tf_op jit(solution)/shard_map/psum | solution.py:81
Sparse Core Ops, SparseCore 0:
  12.7 34.1 reduce-scatter.1
  114.3 14.2 all-gather.1
  138.0 131.3 all-reduce.4
  273.5 100.7 all-reduce.2
where the time goes:
time: 392 us; the launch traced here: 390 us
  waiting for transfers between devices  237 us (60%)
  other arithmetic  52.9 us (13%)
  local copies, waits for them, and re-layouts  50.5 us (13%)
  starting transfers between devices  15.9 us (4%)
  between operations  14 us (4%)
  matrix products  11.2 us (3%)
  blocking collectives  9.29 us (2%)
    psum x1, waiting for transfers between devices, on_device(): two_sum = lax.psum(two_sum, ('feat', 'dom'))  126 us
    psum x1, waiting for transfers between devices, on_device(): one_sum = lax.psum(one_sum.astype(jnp.bfloat16), 'dom').astype(jnp.float32)  102 us
    scatter-add x2, other arithmetic, gather_back(): jnp.zeros((nodes + sends.size, span), jnp.float32).at[nbrs.reshape(-1)]  27.3 us
    all_to_all x3, starting transfers between devices, trade(): lax.all_to_all(buffer, 'dom', split_axis=0, concat_axis=0, tiled=True)  15.5 us
    mul x4, local copies, waits for them, and re-layouts, gather_back(): terms = (weight[..., None] * grads[:, None, :]).reshape(-1, span)  14.2 us
    gather x2, local copies, waits for them, and re-layouts, spread(): gathered = table[nbrs]  9.43 us
    unnamed x28, local copies, waits for them, and re-layouts  9.37 us
    all_to_all x1, blocking collectives, trade(): lax.all_to_all(buffer, 'dom', split_axis=0, concat_axis=0, tiled=True)  9.29 us
  transfers between devices with their start and end apart: 7, of which 5 were waited for; matrix products, arithmetic and copies ran while one was open for 15% of the time, Pallas kernels for 0%

commit v1 on v0

v1 whole, which is shorter than its diff:
```python
import functools
import math

import jax
import jax.numpy as jnp
from jax import lax
from jax.experimental import pallas as pl
from jax.experimental.pallas import tpu as pltpu
from jax.sharding import PartitionSpec as P

BF = jnp.bfloat16
F32 = jnp.float32
SLOT = 16
TILE = 256


def dot(a, b):
    return jnp.dot(a, b, preferred_element_type=F32)


def dot_nt(a, b):
    return lax.dot_general(a, b, (((1,), (1,)), ((), ())), preferred_element_type=F32)


def kernel(
    feat, nx, nz, kmax,
    feats, w_one, w_two, nbr, inv, sidx, grads,
    out, one, two,
    proj, projb, r1, q, qb, r2, cm, ct, sm, st, t1, t2, b1, b2, k0, k1, h0, h1,
    dcs, dh, pself, dnl, joined, ft, dp, g, rx, sx, rz, ts, u1, ub, u2, v, vx, vs, vz,
    ssem, rsem,
):
    ny = feat // 2
    parts = nx * nz
    n = nbr.shape[0]
    w = grads.shape[1]
    cols = w_one.shape[0]
    fan = nbr.shape[1]
    fi = lax.axis_index("feat")
    di = lax.axis_index("dom")
    y, c = fi // 2, fi % 2
    z, x = di // nx, di % nx
    mate = (y * 2 + 1 - c, di)
    count = [0]

    def send(src, dst, device):
        k = count[0]
        count[0] += 1
        copy = pltpu.make_async_remote_copy(
            src_ref=src, dst_ref=dst, send_sem=ssem.at[k], recv_sem=rsem.at[k],
            device_id=device, device_id_type=pl.DeviceIdType.MESH,
        )
        copy.start()
        copies.append(copy)
        return copy

    copies = []
    ypeers = [(lax.rem(y + o, ny) * 2 + c, di) for o in range(1, ny)]
    dpeers = [lax.rem(di + o, parts) for o in range(1, parts)]
    xpeers = [lax.rem(x + o, nx) for o in range(1, nx)]
    zpeers = [lax.rem(z + o, nz) for o in range(1, nz)]

    barrier = pltpu.get_barrier_semaphore()
    everyone = [mate] + ypeers + [(fi, p) for p in dpeers]
    for device in everyone:
        pl.semaphore_signal(barrier, inc=1, device_id=device, device_id_type=pl.DeviceIdType.MESH)

    flat = feats[...].reshape(feat * n, cols)

    def project(h):
        for t in range(w // TILE):
            acc = dot(flat, w_one[:, h * w + t * TILE : h * w + (t + 1) * TILE])
            for f in range(feat):
                part = acc[f * n : (f + 1) * n]
                rows = slice((f // 2) * n, (f // 2 + 1) * n)
                lanes = slice(t * TILE, (t + 1) * TILE)
                proj[h, f % 2, rows, lanes] = part
                projb[h, f % 2, rows, lanes] = part.astype(BF)

    def core_send(h):
        return send(projb.at[h, 1 - c], r1.at[h], mate)

    def y_send(h):
        for j in range(ny):
            rows = slice(j * n, (j + 1) * n)
            qb[h, j] = (proj[h, c, rows] + r1[h, rows].astype(F32)).astype(BF)
        mine = pl.ds(pl.multiple_of(y * n, n), n)
        q[h] = proj[h, c, mine] + r1[h, mine].astype(F32)
        return [
            send(qb.at[h, lax.rem(y + o, ny)], r2.at[h, o - 1], ypeers[o - 1])
            for o in range(1, ny)
        ]

    def owned(h):
        total = q[h]
        for o in range(ny - 1):
            total = total + r2[h, o].astype(F32)
        return total

    def wait(items):
        for item in items:
            item.wait_recv()

    def slot(p):
        return pl.ds(pl.multiple_of(p * SLOT, SLOT), SLOT)

    def table_slot(p):
        return pl.ds(pl.multiple_of(n + p * SLOT, SLOT), SLOT)

    def trade_rows(values, boxes, table):
        table[:n] = values
        boxes[...] = dot(sm[...], values).astype(BF)
        table[table_slot(di)] = boxes[slot(di)]
        return [send(boxes.at[slot(p)], table.at[table_slot(di)], (fi, p)) for p in dpeers]

    def trade_back(values, outgoing, returned):
        terms = dot(ct[...], (values * inv[...]).astype(BF))
        outgoing[...] = terms[n:].astype(BF)
        returned[slot(di)] = outgoing[slot(di)]
        moves = [send(outgoing.at[slot(p)], returned.at[slot(di)], (fi, p)) for p in dpeers]
        return terms[:n], moves

    def gather_start(h):
        block = dp.at[fi, :, h * w : (h + 1) * w]
        return [send(block, block, device) for device in ypeers], send(block, block, mate)

    def gather_forward(h, moves):
        across = []
        for o in range(1, ny):
            moves[o - 1].wait_recv()
            source = lax.rem(y - o + ny, ny) * 2 + c
            block = dp.at[source, :, h * w : (h + 1) * w]
            across.append(send(block, block, mate))
        return across

    project(1)
    pl.semaphore_wait(barrier, len(everyone))
    near_core = core_send(1)
    project(0)
    self_core = core_send(0)
    near_core.wait_recv()
    near_y = y_send(1)
    self_core.wait_recv()
    self_y = y_send(0)

    col = lax.broadcasted_iota(jnp.int32, (n, n + parts * SLOT), 1)
    extra = col - n
    code = jnp.where(
        col < n, col, jnp.where(extra % SLOT < kmax, n + (extra // SLOT) * kmax + extra % SLOT, -2)
    )
    counts = jnp.zeros(code.shape, F32)
    for s in range(fan):
        counts = counts + jnp.where(nbr[:, s : s + 1] == code, 1.0, 0.0)
    cm[...] = counts.astype(BF)
    ct[...] = counts.T.astype(BF)
    picks = jnp.where(
        sidx[...] == lax.broadcasted_iota(jnp.int32, (parts * SLOT, n), 1), 1.0, 0.0
    )
    sm[...] = picks.astype(BF)
    st[...] = picks.T.astype(BF)
    dcat = dot_nt(grads[...], w_two[...])
    dcs[...] = dcat[:, :w]
    local, back_agg = trade_back(dcat[:, w:], k0, h0)
    dcs[...] += local
    ft[...] = flat.T

    wait(near_y)
    rows_near = trade_rows(owned(1).astype(BF), b1, t1)
    wait(self_y)
    pself[...] = owned(0)
    wait(back_agg)
    dh[...] = dcs[...] + dot(st[...], h0[...])
    wait(rows_near)
    pre = pself[...] + dot(cm[...], t1[...]) * inv[...]
    sig = 1.0 / (1.0 + jnp.exp(-pre))
    d_pre = dh[...] * sig * (1.0 + pre * (1.0 - sig))
    dp[fi, :, :w] = d_pre.astype(BF)
    near_local, back_pre = trade_back(d_pre, k1, h1)
    dnl[...] = near_local
    gather0, across0 = gather_start(0)
    hidden = (pre * sig).astype(BF)
    joined[:, :w] = hidden
    rows_hidden = trade_rows(hidden, b2, t2)

    wait(back_pre)
    dp[fi, :, w:] = (dnl[...] + dot(st[...], h1[...])).astype(BF)
    gather1, across1 = gather_start(1)
    forward0 = gather_forward(0, gather0)

    wait(rows_hidden)
    agg = dot(cm[...], t2[...]) * inv[...]
    joined[:, w:] = agg.astype(BF)
    both = joined[...]
    out[0] = dot(both, w_two[...]).astype(BF)
    span = two.shape[0] // feat
    two_part = dot(both.T, grads[...]).astype(BF)
    for f in range(feat):
        ts[f % 2, (f // 2) * span : (f // 2 + 1) * span] = two_part[f * span : (f + 1) * span]
    two_core = send(ts.at[1 - c], u1, mate)

    forward1 = gather_forward(1, gather1)

    rows_x = cols // nx
    rows_z = rows_x // nz

    def lanes_of(k):
        return slice(k * TILE, (k + 1) * TILE)

    def chunk(k):
        lanes = lanes_of(k)
        g[:, lanes] = dot(ft[...], dp[:, :, lanes].reshape(feat * n, TILE)).astype(BF)
        return [
            send(g.at[pl.ds(pl.multiple_of(t * rows_x, SLOT), rows_x), lanes],
                 rx.at[o, :, lanes], (fi, z * nx + t))
            for o, t in enumerate(xpeers)
        ]

    def z_scatter(k, moves):
        wait(moves)
        lanes = lanes_of(k)
        total = g[pl.ds(pl.multiple_of(x * rows_x, SLOT), rows_x), lanes].astype(F32)
        for o in range(nx - 1):
            total = total + rx[o, :, lanes].astype(F32)
        sx[:, lanes] = total.astype(BF)
        return [
            send(sx.at[pl.ds(pl.multiple_of(t * rows_z, SLOT), rows_z), lanes],
                 rz.at[o, :, lanes], (fi, t * nx + x))
            for o, t in enumerate(zpeers)
        ]

    def z_gather(k, moves):
        wait(moves)
        lanes = lanes_of(k)
        total = sx[pl.ds(pl.multiple_of(z * rows_z, SLOT), rows_z), lanes].astype(F32)
        for o in range(nz - 1):
            total = total + rz[o, :, lanes].astype(F32)
        mine = pl.ds(pl.multiple_of(x * rows_x + z * rows_z, SLOT), rows_z)
        one[mine, lanes] = total.astype(BF)
        piece = one.at[mine, lanes]
        return [send(piece, piece, (fi, t * nx + x)) for t in zpeers]

    def x_gather(k, moves):
        wait(moves)
        piece = one.at[pl.ds(pl.multiple_of(x * rows_x, SLOT), rows_x), lanes_of(k)]
        return [send(piece, piece, (fi, z * nx + t)) for t in xpeers]

    lanes_x = w // nx
    span_z = span // nz
    my_lanes = pl.ds(pl.multiple_of(x * lanes_x, 128), lanes_x)

    def two_y():
        two_core.wait_recv()
        ub[...] = (ts[c].astype(F32) + u1[...].astype(F32)).astype(BF)
        return [
            send(ub.at[pl.ds(pl.multiple_of(lax.rem(y + o, ny) * span, SLOT), span)],
                 u2.at[o - 1], ypeers[o - 1])
            for o in range(1, ny)
        ]

    def two_x(moves):
        wait(moves)
        total = ub[pl.ds(pl.multiple_of(y * span, SLOT), span)].astype(F32)
        for o in range(ny - 1):
            total = total + u2[o].astype(F32)
        for t in range(nx):
            v[t] = total[:, t * lanes_x : (t + 1) * lanes_x].astype(BF)
        return [send(v.at[t], vx.at[o], (fi, z * nx + t)) for o, t in enumerate(xpeers)]

    def two_z(moves):
        wait(moves)
        total = v[x].astype(F32)
        for o in range(nx - 1):
            total = total + vx[o].astype(F32)
        vs[...] = total.astype(BF)
        return [
            send(vs.at[pl.ds(pl.multiple_of(t * span_z, SLOT), span_z)], vz.at[o], (fi, t * nx + x))
            for o, t in enumerate(zpeers)
        ]

    def two_zg(moves):
        wait(moves)
        total = vs[pl.ds(pl.multiple_of(z * span_z, SLOT), span_z)].astype(F32)
        for o in range(nz - 1):
            total = total + vz[o].astype(F32)
        mine = pl.ds(pl.multiple_of(fi * span + z * span_z, SLOT), span_z)
        two[mine, my_lanes] = total.astype(BF)
        piece = two.at[mine, my_lanes]
        return [send(piece, piece, (fi, t * nx + x)) for t in zpeers]

    def two_xg(moves):
        wait(moves)
        piece = two.at[pl.ds(pl.multiple_of(fi * span, SLOT), span), my_lanes]
        return [send(piece, piece, (fi, z * nx + t)) for t in xpeers]

    def two_yg(moves):
        wait(moves)
        piece = two.at[pl.ds(pl.multiple_of(fi * span, SLOT), span)]
        return [send(piece, piece, device) for device in ypeers], send(piece, piece, mate)

    def two_across(moves):
        across = []
        for o in range(1, ny):
            moves[o - 1].wait_recv()
            source = lax.rem(y - o + ny, ny) * 2 + c
            piece = two.at[pl.ds(pl.multiple_of(source * span, SLOT), span)]
            across.append(send(piece, piece, mate))
        return across

    chunks = 2 * w // TILE
    half = chunks // 2
    moves = {}
    two_moves = two_y()
    across0.wait_recv()
    wait(forward0)
    for k in range(half):
        moves[k] = chunk(k)
    two_moves = two_x(two_moves)
    across1.wait_recv()
    wait(forward1)
    for k in range(half, chunks):
        moves[k] = chunk(k)
    stages = [z_scatter, z_gather, x_gather]
    two_stages = [two_z, two_zg, two_xg]
    for step in range(chunks + len(stages) - 1):
        for s in reversed(range(len(stages))):
            k = step - s
            if 0 <= k < chunks:
                moves[k] = stages[s](k, moves[k])
        if step < len(two_stages):
            two_moves = two_stages[step](two_moves)
        elif step == len(two_stages):
            two_moves, two_mate = two_yg(two_moves)
        elif step == len(two_stages) + 1:
            two_moves = two_across(two_moves)
    for k in range(chunks):
        wait(moves[k])
    wait(two_moves)
    two_mate.wait_recv()
    for copy in copies:
        copy.wait_send()


def on_device(nx, nz, features, w_one, w_two, neighbor, degree, send_rows, grad_out):
    feat, n, cols = features.shape
    w = w_two.shape[1]
    ny = feat // 2
    parts, kmax = send_rows.shape[1:]
    fan = neighbor.shape[2]
    slots = jnp.arange(fan, dtype=jnp.int32)
    nbr = jnp.where(slots[None, :] < degree[0][:, None], neighbor[0], -1)
    inv = 1.0 / degree[0].astype(F32)[:, None]
    sidx = jnp.pad(send_rows[0], ((0, 0), (0, SLOT - kmax)), constant_values=-1).reshape(-1, 1)
    table = n + parts * SLOT
    edge = parts * SLOT
    rows_x = cols // nx
    rows_z = rows_x // nz
    span = 2 * w // feat
    lanes_x = w // nx
    chunks = 2 * w // TILE
    n_copies = (
        2 + 4 * (ny - 1) + 4 * (parts - 1) + 2 + 2 * (ny - 1)
        + chunks * 2 * (nx - 1 + nz - 1)
        + 1 + (ny - 1) + 2 * (nx - 1 + nz - 1) + 2 * (ny - 1) + 1
    )
    vm = pltpu.VMEM
    scratch = [
        vm((2, 2, ny * n, w), F32), vm((2, 2, ny * n, w), BF), vm((2, ny * n, w), BF),
        vm((2, n, w), F32), vm((2, ny, n, w), BF), vm((2, ny - 1, n, w), BF),
        vm((n, table), BF), vm((table, n), BF), vm((edge, n), BF), vm((n, edge), BF),
        vm((table, w), BF), vm((table, w), BF), vm((edge, w), BF), vm((edge, w), BF),
        vm((edge, w), BF), vm((edge, w), BF), vm((edge, w), BF), vm((edge, w), BF),
        vm((n, w), F32), vm((n, w), F32), vm((n, w), F32), vm((n, w), F32),
        vm((n, 2 * w), BF), vm((cols, feat * n), BF), vm((feat, n, 2 * w), BF),
        vm((cols, 2 * w), BF), vm((nx - 1, rows_x, 2 * w), BF), vm((rows_x, 2 * w), BF),
        vm((nz - 1, rows_z, 2 * w), BF),
        vm((2, ny * span, w), BF), vm((ny * span, w), BF), vm((ny * span, w), BF),
        vm((ny - 1, span, w), BF), vm((nx, span, lanes_x), BF), vm((nx - 1, span, lanes_x), BF),
        vm((span, lanes_x), BF), vm((nz - 1, span // nz, lanes_x), BF),
        pltpu.SemaphoreType.DMA((n_copies,)), pltpu.SemaphoreType.DMA((n_copies,)),
    ]
    spec = pl.BlockSpec(memory_space=pltpu.VMEM)
    out, one_sum, two_sum = pl.pallas_call(
        functools.partial(kernel, feat, nx, nz, kmax),
        out_shape=(
            jax.ShapeDtypeStruct((1, n, w), BF),
            jax.ShapeDtypeStruct((cols, 2 * w), BF),
            jax.ShapeDtypeStruct((2 * w, w), BF),
        ),
        in_specs=[spec] * 7,
        out_specs=(spec, spec, spec),
        scratch_shapes=scratch,
        compiler_params=pltpu.CompilerParams(
            collective_id=0, has_side_effects=True, vmem_limit_bytes=56 * 1024 * 1024
        ),
    )(features, w_one, w_two, nbr, inv, sidx, grad_out[0])
    scale = 1.0 / math.sqrt(feat * n * parts)
    return out, one_sum.astype(F32) * scale, two_sum.astype(F32) * scale


def solution(mesh):
    parts = mesh.shape["dom"]
    nx = 1 << ((parts.bit_length() - 2) // 2)
    in_specs = (
        P(None, "dom", "feat"),
        P("feat", None),
        P(),
        P("feat", "dom", None),
        P("feat", "dom"),
        P("feat", "dom", None),
        P("feat", "dom", None),
    )
    out_specs = (P("feat", "dom", None), P("feat", None), P())
    return jax.shard_map(
        functools.partial(on_device, nx, parts // nx),
        mesh=mesh, in_specs=in_specs, out_specs=out_specs, check_vma=False,
    )
```

time: 392 us -> 117 us (0.30)
  waiting for transfers between devices: 237 us -> 0 us
  Pallas kernels: 0 us -> 105 us
  local copies, waits for them, and re-layouts: 50.5 us -> 3.61 us
  other arithmetic: 52.9 us -> 7.92 us
  starting transfers between devices: 15.9 us -> 0 us
  between operations: 14 us -> 0.65 us
  matrix products: 11.2 us -> 0 us
  blocking collectives: 9.29 us -> 0 us
    psum x2 -> x0, waiting for transfers between devices: 228 us -> none  [the longest x1 126 us: on_device(): two_sum = lax.psum(two_sum, ('feat', 'dom'))]
    pallas_call x0 -> x1, Pallas kernels: none -> 105 us  [on_device(): pl.pallas_call(functools.partial(kernel, feat, nx, nz, kmax), out_shape=(...]
    scatter-add x4 -> x0, other arithmetic: 32.7 us -> none  [the longest x2 27.3 us: gather_back(): jnp.zeros((nodes + sends.size, span), jnp.float32).at[nbrs.reshape(-1)]]
    all_to_all x3 -> x0, starting transfers between devices: 15.5 us -> none  [trade(): lax.all_to_all(buffer, 'dom', split_axis=0, concat_axis=0, tiled=True)]
    mul x4 -> x0, local copies, waits for them, and re-layouts: 14.2 us -> none  [gather_back(): terms = (weight[..., None] * grads[:, None, :]).reshape(-1, span)]
    gather x4 -> x0, local copies, waits for them, and re-layouts: 11.6 us -> none  [the longest x2 9.43 us: spread(): gathered = table[nbrs]]
    dot_general x5 -> x0, matrix products: 11.2 us -> none  [the longest x1 4.15 us: on_device(): lax.dot_general(rows, lax.all_gather(d_proj, 'feat', axis=0, tiled=True),...]
    all_to_all x1 -> x0, blocking collectives: 9.29 us -> none  [trade(): lax.all_to_all(buffer, 'dom', split_axis=0, concat_axis=0, tiled=True)]
  transfers between devices with their start and end apart: 7 -> 0, of which waited for: 5 -> 0; matrix products, arithmetic and copies ran while one was open for 15% -> 0% of each run, Pallas kernels for 0% -> 0%
where the time goes in v1:
time: 117 us
  Pallas kernels  105 us (90%)
  other arithmetic  7.92 us (7%)
  local copies, waits for them, and re-layouts  3.61 us (3%)
    pallas_call x1, Pallas kernels, on_device(): pl.pallas_call(functools.partial(kernel, feat, nx, nz, kmax), out_shape=(...  105 us
    mul x2, other arithmetic, on_device(): return (out, one_sum.astype(F32) * scale, two_sum.astype(F32) * scale)  5.9 us

profile of v1, /device:TPU:0, one launch (start us, length us, event | category | flops | bytes accessed | tf_op | source)
XLA Modules:
  0.0 116.8 jit_solution(2630621536463537876)
XLA Ops:
  0.6 0.8 copy.10
  1.4 1.4 %bitcast_select_fusion.nbr = s32[128,10]{1,0:T(8,128)} fusion(s32[1,128,10]{2,1,0:T(8,128)S(1)} %copy.10, s32[128]{0:T(128)} %bitcast.9), kind=kLoop, calls=%fused_computation.2 | loop fusion | flops 2560 | bytes 10752 | tf_op jit(solution)/shard_map/jit(_where)/select_n | solution.py:350
  2.8 0.7 pad.4
  3.5 0.7 reshape.28.sidx
  4.2 0.7 divide_bitcast_fusion
  4.9 0.7 copy.11.inv
  5.6 104.7 %shard_map.94 = (bf16[1,128,512]{2,1,0:T(8,128)(2,1)}, bf16[1024,1024]{1,0:T(8,128)(2,1)}, bf16[1024,512]{1,0:T(8,128)(2,1)}) custom-call(bf16[4,128,1024]{2,1,0:T(8,128)(2,1)} %feats.1, bf16[1024,1024]{1,0:T(8,128)(2,1)} %w_one.1, bf16[1024,512]{1,0:T(8,128)(2,1)} %w_two.1, s32[128,10]{1,0:T(8,128)} %bitcast_select_fusion.nbr, f32[128,1]{1,0:T(8,128)} %copy.11.inv, ...), custom_call_target="tpu_custom_call" | custom-call | tf_op jit(solution)/shard_map/pallas_call | solution.py:382
  110.3 0.0 copy-start
  110.3 4.3 %convert_multiply_fusion = f32[1024,1024]{1,0:T(8,128)} fusion(bf16[1024,1024]{1,0:T(8,128)(2,1)} %get-tuple-element.7), kind=kLoop, calls=%fused_computation | loop fusion | flops 2097152 | bytes 6291456 | tf_op jit(solution)/shard_map/mul | solution.py:397
  114.6 0.0 copy-start.1
  114.6 0.0 copy-done
  114.6 1.6 %convert_multiply_fusion.1 = f32[1024,512]{1,0:T(8,128)} fusion(bf16[1024,512]{1,0:T(8,128)(2,1)S(1)} %copy-done), kind=kLoop, calls=%fused_computation.1 | loop fusion | flops 1048576 | bytes 3145728 | tf_op jit(solution)/shard_map/mul | solution.py:397
  116.2 0.0 copy-done.1
  116.2 0.7 copy.14
Async XLA Ops:
  110.3 4.3 %copy-start = (bf16[1024,512]{1,0:T(8,128)(2,1)S(1)}, bf16[1024,512]{1,0:T(8,128)(2,1)}, u32[]{:S(2)}) copy-start(bf16[1024,512]{1,0:T(8,128)(2,1)} %get-tuple-element.8) | copy-start | bytes 3145732
  114.6 1.6 %copy-start.1 = (bf16[1,128,512]{2,1,0:T(8,128)(2,1)S(1)}, bf16[1,128,512]{2,1,0:T(8,128)(2,1)}, u32[]{:S(2)}) copy-start(bf16[1,128,512]{2,1,0:T(8,128)(2,1)} %get-tuple-element.12) | copy-start | bytes 393220

commit v2 on v1

--- a/solution.py
+++ b/solution.py
@@ -24,23 +24,26 @@
 
 def kernel(
     feat, nx, nz, kmax,
-    feats, w_one, w_two, nbr, inv, sidx, grads,
+    feats, w_one, w_two, nbr, deg, sends, grads,
     out, one, two,
     proj, projb, r1, q, qb, r2, cm, ct, sm, st, t1, t2, b1, b2, k0, k1, h0, h1,
-    dcs, dh, pself, dnl, joined, ft, dp, g, rx, sx, rz, ts, u1, ub, u2, v, vx, vs, vz,
+    inv, dcs, dh, pself, dnl, joined, fx, ft, dp, g, rx, sx, rz, ts, u1, ub, u2, v, vx, vs, vz,
     ssem, rsem,
 ):
     ny = feat // 2
     parts = nx * nz
-    n = nbr.shape[0]
+    n = nbr.shape[1]
     w = grads.shape[1]
     cols = w_one.shape[0]
-    fan = nbr.shape[1]
+    fan = nbr.shape[0]
+    half_cols = cols // 2
     fi = lax.axis_index("feat")
     di = lax.axis_index("dom")
     y, c = fi // 2, fi % 2
     z, x = di // nx, di % nx
     mate = (y * 2 + 1 - c, di)
+    zlow, zhigh = z % 2, z // 2
+    pair = (fi, (z + 1 - 2 * zlow) * nx + x)
     count = [0]
 
     def send(src, dst, device):
@@ -58,7 +61,7 @@
     ypeers = [(lax.rem(y + o, ny) * 2 + c, di) for o in range(1, ny)]
     dpeers = [lax.rem(di + o, parts) for o in range(1, parts)]
     xpeers = [lax.rem(x + o, nx) for o in range(1, nx)]
-    zpeers = [lax.rem(z + o, nz) for o in range(1, nz)]
+    zpeers = [lax.rem(zhigh + o, nz // 2) * 2 + zlow for o in range(1, nz // 2)]
 
     barrier = pltpu.get_barrier_semaphore()
     everyone = [mate] + ypeers + [(fi, p) for p in dpeers]
@@ -120,22 +123,47 @@
         moves = [send(outgoing.at[slot(p)], returned.at[slot(di)], (fi, p)) for p in dpeers]
         return terms[:n], moves
 
+    def block(low, f, h):
+        return dp.at[low, f, :, h * w : (h + 1) * w]
+
+    def pass_on(low, f, h, device):
+        return send(block(low, f, h), block(low, f, h), device)
+
+    def y_source(o):
+        return lax.rem(y - o + ny, ny) * 2 + c
+
     def gather_start(h):
-        block = dp.at[fi, :, h * w : (h + 1) * w]
-        return [send(block, block, device) for device in ypeers], send(block, block, mate)
-
-    def gather_forward(h, moves):
-        across = []
+        to_pair = pass_on(zlow, fi, h, pair)
+        to_y = [pass_on(zlow, fi, h, device) for device in ypeers]
+        return to_pair, to_y, [pass_on(zlow, fi, h, mate)]
+
+    def gather_y_first(h, to_pair, to_y, to_mate):
+        paired = [to_pair]
         for o in range(1, ny):
-            moves[o - 1].wait_recv()
-            source = lax.rem(y - o + ny, ny) * 2 + c
-            block = dp.at[source, :, h * w : (h + 1) * w]
-            across.append(send(block, block, mate))
-        return across
+            to_y[o - 1].wait_recv()
+            paired.append(pass_on(zlow, y_source(o), h, pair))
+            to_mate.append(pass_on(zlow, y_source(o), h, mate))
+        for o in range(ny):
+            paired[o].wait_recv()
+            to_mate.append(pass_on(1 - zlow, y_source(o), h, mate))
+        return to_mate
+
+    def gather_pair_first(h, to_pair, to_y, to_mate):
+        to_pair.wait_recv()
+        far = [pass_on(1 - zlow, fi, h, device) for device in ypeers]
+        to_mate.append(pass_on(1 - zlow, fi, h, mate))
+        for low, moves in ((zlow, to_y), (1 - zlow, far)):
+            for o in range(1, ny):
+                moves[o - 1].wait_recv()
+                to_mate.append(pass_on(low, y_source(o), h, mate))
+        return to_mate
 
     project(1)
     pl.semaphore_wait(barrier, len(everyone))
     near_core = core_send(1)
+    far_cols = pl.ds(pl.multiple_of((1 - zlow) * half_cols, 128), half_cols)
+    near_cols = pl.ds(pl.multiple_of(zlow * half_cols, 128), half_cols)
+    features_move = send(feats.at[:, :, far_cols], fx, pair)
     project(0)
     self_core = core_send(0)
     near_core.wait_recv()
@@ -143,26 +171,35 @@
     self_core.wait_recv()
     self_y = y_send(0)
 
-    col = lax.broadcasted_iota(jnp.int32, (n, n + parts * SLOT), 1)
-    extra = col - n
+    eye = lax.broadcasted_iota(jnp.int32, (n, n), 0) == lax.broadcasted_iota(jnp.int32, (n, n), 1)
+    inv[...] = 1.0 / jnp.sum(jnp.where(eye, deg[...].astype(F32), 0.0), axis=1, keepdims=True)
+    entry = lax.broadcasted_iota(jnp.int32, (n + parts * SLOT, n), 0)
+    extra = entry - n
     code = jnp.where(
-        col < n, col, jnp.where(extra % SLOT < kmax, n + (extra // SLOT) * kmax + extra % SLOT, -2)
+        entry < n, entry,
+        jnp.where(extra % SLOT < kmax, n + (extra // SLOT) * kmax + extra % SLOT, -2),
     )
     counts = jnp.zeros(code.shape, F32)
     for s in range(fan):
-        counts = counts + jnp.where(nbr[:, s : s + 1] == code, 1.0, 0.0)
-    cm[...] = counts.astype(BF)
-    ct[...] = counts.T.astype(BF)
-    picks = jnp.where(
-        sidx[...] == lax.broadcasted_iota(jnp.int32, (parts * SLOT, n), 1), 1.0, 0.0
-    )
+        used = jnp.where(s < deg[...], nbr[s : s + 1], -1)
+        counts = counts + jnp.where(used == code, 1.0, 0.0)
+    ct[...] = counts.astype(BF)
+    cm[...] = counts.T.astype(BF)
+    edge = (parts * SLOT, parts)
+    owner = lax.broadcasted_iota(jnp.int32, edge, 0) // SLOT == lax.broadcasted_iota(jnp.int32, edge, 1)
+    spread_rows = dot(jnp.where(owner, 1.0, 0.0).astype(BF), sends[...].astype(F32).astype(BF))
+    place = (parts * SLOT, kmax)
+    here = lax.broadcasted_iota(jnp.int32, place, 0) % SLOT == lax.broadcasted_iota(jnp.int32, place, 1)
+    chosen = jnp.sum(jnp.where(here, spread_rows + 1.0, 0.0), axis=1, keepdims=True) - 1.0
+    lane = lax.broadcasted_iota(jnp.int32, (parts * SLOT, n), 1).astype(F32)
+    picks = jnp.where(chosen == lane, 1.0, 0.0)
     sm[...] = picks.astype(BF)
     st[...] = picks.T.astype(BF)
     dcat = dot_nt(grads[...], w_two[...])
     dcs[...] = dcat[:, :w]
     local, back_agg = trade_back(dcat[:, w:], k0, h0)
     dcs[...] += local
-    ft[...] = flat.T
+    ft[zlow] = feats[:, :, near_cols].reshape(feat * n, half_cols).T
 
     wait(near_y)
     rows_near = trade_rows(owned(1).astype(BF), b1, t1)
@@ -174,18 +211,19 @@
     pre = pself[...] + dot(cm[...], t1[...]) * inv[...]
     sig = 1.0 / (1.0 + jnp.exp(-pre))
     d_pre = dh[...] * sig * (1.0 + pre * (1.0 - sig))
-    dp[fi, :, :w] = d_pre.astype(BF)
+    dp[zlow, fi, :, :w] = d_pre.astype(BF)
     near_local, back_pre = trade_back(d_pre, k1, h1)
     dnl[...] = near_local
-    gather0, across0 = gather_start(0)
+    gather0 = gather_start(0)
     hidden = (pre * sig).astype(BF)
     joined[:, :w] = hidden
     rows_hidden = trade_rows(hidden, b2, t2)
 
     wait(back_pre)
-    dp[fi, :, w:] = (dnl[...] + dot(st[...], h1[...])).astype(BF)
-    gather1, across1 = gather_start(1)
-    forward0 = gather_forward(0, gather0)
+    dp[zlow, fi, :, w:] = (dnl[...] + dot(st[...], h1[...])).astype(BF)
+    gather1 = gather_start(1)
+    features_move.wait_recv()
+    ft[1 - zlow] = fx[...].reshape(feat * n, half_cols).T
 
     wait(rows_hidden)
     agg = dot(cm[...], t2[...]) * inv[...]
@@ -198,17 +236,21 @@
         ts[f % 2, (f // 2) * span : (f // 2 + 1) * span] = two_part[f * span : (f + 1) * span]
     two_core = send(ts.at[1 - c], u1, mate)
 
-    forward1 = gather_forward(1, gather1)
-
-    rows_x = cols // nx
-    rows_z = rows_x // nz
+    arrived0 = gather_y_first(0, *gather0)
+    arrived1 = gather_pair_first(1, *gather1)
+
+    rows_x = half_cols // nx
+    rows_z = rows_x // (nz // 2)
 
     def lanes_of(k):
         return slice(k * TILE, (k + 1) * TILE)
 
     def chunk(k):
         lanes = lanes_of(k)
-        g[:, lanes] = dot(ft[...], dp[:, :, lanes].reshape(feat * n, TILE)).astype(BF)
+        g[:, lanes] = (
+            dot(ft[0], dp[0, :, :, lanes].reshape(feat * n, TILE))
+            + dot(ft[1], dp[1, :, :, lanes].reshape(feat * n, TILE))
+        ).astype(BF)
         return [
             send(g.at[pl.ds(pl.multiple_of(t * rows_x, SLOT), rows_x), lanes],
                  rx.at[o, :, lanes], (fi, z * nx + t))
@@ -223,29 +265,49 @@
             total = total + rx[o, :, lanes].astype(F32)
         sx[:, lanes] = total.astype(BF)
         return [
-            send(sx.at[pl.ds(pl.multiple_of(t * rows_z, SLOT), rows_z), lanes],
+            send(sx.at[pl.ds(pl.multiple_of((t // 2) * rows_z, SLOT), rows_z), lanes],
                  rz.at[o, :, lanes], (fi, t * nx + x))
             for o, t in enumerate(zpeers)
         ]
 
+    def piece(k, low, at):
+        return one.at[pl.ds(pl.multiple_of(low * half_cols + at * rows_x, SLOT), rows_x), lanes_of(k)]
+
     def z_gather(k, moves):
         wait(moves)
         lanes = lanes_of(k)
-        total = sx[pl.ds(pl.multiple_of(z * rows_z, SLOT), rows_z), lanes].astype(F32)
-        for o in range(nz - 1):
+        total = sx[pl.ds(pl.multiple_of(zhigh * rows_z, SLOT), rows_z), lanes].astype(F32)
+        for o in range(nz // 2 - 1):
             total = total + rz[o, :, lanes].astype(F32)
-        mine = pl.ds(pl.multiple_of(x * rows_x + z * rows_z, SLOT), rows_z)
+        mine = pl.ds(
+            pl.multiple_of(zlow * half_cols + x * rows_x + zhigh * rows_z, SLOT), rows_z
+        )
         one[mine, lanes] = total.astype(BF)
-        piece = one.at[mine, lanes]
-        return [send(piece, piece, (fi, t * nx + x)) for t in zpeers]
-
-    def x_gather(k, moves):
-        wait(moves)
-        piece = one.at[pl.ds(pl.multiple_of(x * rows_x, SLOT), rows_x), lanes_of(k)]
-        return [send(piece, piece, (fi, z * nx + t)) for t in xpeers]
+        return [send(one.at[mine, lanes], one.at[mine, lanes], (fi, t * nx + x)) for t in zpeers]
+
+    def first_gather(k, moves):
+        wait(moves)
+        mine = piece(k, zlow, x)
+        to_x = [send(mine, mine, (fi, z * nx + t)) for t in xpeers]
+        return to_x, send(mine, mine, pair)
+
+    def last_gather(k, moves):
+        to_x, to_pair = moves
+        rest = []
+        if k % 2:
+            to_pair.wait_recv()
+            got = piece(k, 1 - zlow, x)
+            rest = [send(got, got, (fi, z * nx + t)) for t in xpeers]
+            return to_x + rest
+        for o in range(1, nx):
+            to_x[o - 1].wait_recv()
+            got = piece(k, zlow, lax.rem(x - o + nx, nx))
+            rest.append(send(got, got, pair))
+        return [to_pair] + rest
 
     lanes_x = w // nx
     span_z = span // nz
+    allz = [lax.rem(z + o, nz) for o in range(1, nz)]
     my_lanes = pl.ds(pl.multiple_of(x * lanes_x, 128), lanes_x)
 
     def two_y():
@@ -274,7 +336,7 @@
         vs[...] = total.astype(BF)
         return [
             send(vs.at[pl.ds(pl.multiple_of(t * span_z, SLOT), span_z)], vz.at[o], (fi, t * nx + x))
-            for o, t in enumerate(zpeers)
+            for o, t in enumerate(allz)
         ]
 
     def two_zg(moves):
@@ -285,7 +347,7 @@
         mine = pl.ds(pl.multiple_of(fi * span + z * span_z, SLOT), span_z)
         two[mine, my_lanes] = total.astype(BF)
         piece = two.at[mine, my_lanes]
-        return [send(piece, piece, (fi, t * nx + x)) for t in zpeers]
+        return [send(piece, piece, (fi, t * nx + x)) for t in allz]
 
     def two_xg(moves):
         wait(moves)
@@ -310,16 +372,14 @@
     half = chunks // 2
     moves = {}
     two_moves = two_y()
-    across0.wait_recv()
-    wait(forward0)
+    wait(arrived0)
     for k in range(half):
         moves[k] = chunk(k)
     two_moves = two_x(two_moves)
-    across1.wait_recv()
-    wait(forward1)
+    wait(arrived1)
     for k in range(half, chunks):
         moves[k] = chunk(k)
-    stages = [z_scatter, z_gather, x_gather]
+    stages = [z_scatter, z_gather, first_gather, last_gather]
     two_stages = [two_z, two_zg, two_xg]
     for step in range(chunks + len(stages) - 1):
         for s in reversed(range(len(stages))):
@@ -345,22 +405,18 @@
     w = w_two.shape[1]
     ny = feat // 2
     parts, kmax = send_rows.shape[1:]
-    fan = neighbor.shape[2]
-    slots = jnp.arange(fan, dtype=jnp.int32)
-    nbr = jnp.where(slots[None, :] < degree[0][:, None], neighbor[0], -1)
-    inv = 1.0 / degree[0].astype(F32)[:, None]
-    sidx = jnp.pad(send_rows[0], ((0, 0), (0, SLOT - kmax)), constant_values=-1).reshape(-1, 1)
     table = n + parts * SLOT
     edge = parts * SLOT
-    rows_x = cols // nx
-    rows_z = rows_x // nz
+    half_cols = cols // 2
+    rows_x = half_cols // nx
+    rows_z = rows_x // (nz // 2)
     span = 2 * w // feat
     lanes_x = w // nx
     chunks = 2 * w // TILE
     n_copies = (
-        2 + 4 * (ny - 1) + 4 * (parts - 1) + 2 + 2 * (ny - 1)
-        + chunks * 2 * (nx - 1 + nz - 1)
-        + 1 + (ny - 1) + 2 * (nx - 1 + nz - 1) + 2 * (ny - 1) + 1
+        3 + 2 * (ny - 1) + 4 * (parts - 1) + 2 * (2 + 2 * ny) + 4 * ny
+        + chunks * (4 * nx + nz)
+        + 2 + 4 * ny + 2 * (nx + nz)
     )
     vm = pltpu.VMEM
     scratch = [
@@ -369,10 +425,11 @@
         vm((n, table), BF), vm((table, n), BF), vm((edge, n), BF), vm((n, edge), BF),
         vm((table, w), BF), vm((table, w), BF), vm((edge, w), BF), vm((edge, w), BF),
         vm((edge, w), BF), vm((edge, w), BF), vm((edge, w), BF), vm((edge, w), BF),
-        vm((n, w), F32), vm((n, w), F32), vm((n, w), F32), vm((n, w), F32),
-        vm((n, 2 * w), BF), vm((cols, feat * n), BF), vm((feat, n, 2 * w), BF),
-        vm((cols, 2 * w), BF), vm((nx - 1, rows_x, 2 * w), BF), vm((rows_x, 2 * w), BF),
-        vm((nz - 1, rows_z, 2 * w), BF),
+        vm((n, 1), F32), vm((n, w), F32), vm((n, w), F32), vm((n, w), F32), vm((n, w), F32),
+        vm((n, 2 * w), BF), vm((feat, n, half_cols), BF), vm((2, half_cols, feat * n), BF),
+        vm((2, feat, n, 2 * w), BF),
+        vm((half_cols, 2 * w), BF), vm((nx - 1, rows_x, 2 * w), BF), vm((rows_x, 2 * w), BF),
+        vm((nz // 2 - 1, rows_z, 2 * w), BF),
         vm((2, ny * span, w), BF), vm((ny * span, w), BF), vm((ny * span, w), BF),
         vm((ny - 1, span, w), BF), vm((nx, span, lanes_x), BF), vm((nx - 1, span, lanes_x), BF),
         vm((span, lanes_x), BF), vm((nz - 1, span // nz, lanes_x), BF),
@@ -390,9 +447,9 @@
         out_specs=(spec, spec, spec),
         scratch_shapes=scratch,
         compiler_params=pltpu.CompilerParams(
-            collective_id=0, has_side_effects=True, vmem_limit_bytes=56 * 1024 * 1024
+            collective_id=0, has_side_effects=True, vmem_limit_bytes=40 * 1024 * 1024
         ),
-    )(features, w_one, w_two, nbr, inv, sidx, grad_out[0])
+    )(features, w_one, w_two, neighbor[0].T, degree, send_rows[0], grad_out[0])
     scale = 1.0 / math.sqrt(feat * n * parts)
     return out, one_sum.astype(F32) * scale, two_sum.astype(F32) * scale
 

time: 117 us -> 109 us (0.932)
  Pallas kernels: 105 us -> 95.9 us
  local copies, waits for them, and re-layouts: 3.61 us -> 7.63 us
  other arithmetic: 7.92 us -> 4.22 us
    pallas_call x1, Pallas kernels: 105 us -> 95.9 us  [on_device(): pl.pallas_call(functools.partial(kernel, feat, nx, nz, kmax), out_shape=(...]
    unnamed x6 -> x14, local copies, waits for them, and re-layouts: 1.46 us -> 7.63 us
    mul x2, other arithmetic: 5.9 us -> 4.22 us  [on_device(): return (out, one_sum.astype(F32) * scale, two_sum.astype(F32) * scale)]
    select_n x1 -> x0, other arithmetic: 1.37 us -> none  [on_device(): nbr = jnp.where(slots[None, :] < degree[0][:, None], neighbor[0], -1)]
where the time goes in v2:
time: 109 us; the launch traced here: 108 us
  Pallas kernels  95.9 us (88%)
  local copies, waits for them, and re-layouts  7.63 us (7%)
  other arithmetic  4.22 us (4%)
    pallas_call x1, Pallas kernels, on_device(): pl.pallas_call(functools.partial(kernel, feat, nx, nz, kmax), out_shape=(...  95.9 us
    unnamed x14, local copies, waits for them, and re-layouts  7.63 us
    mul x2, other arithmetic, on_device(): return (out, one_sum.astype(F32) * scale, two_sum.astype(F32) * scale)  4.22 us

profile of v2, /device:TPU:0, one launch (start us, length us, event | category | flops | bytes accessed | tf_op | source)
XLA Modules:
  0.0 108.4 jit_solution(16235194887174635258)
XLA Ops:
  0.6 0.7 copy.12
  1.3 0.0 copy-start
  1.3 1.6 %copy-done = bf16[1024,1024]{1,0:T(8,128)(2,1)S(1)} copy-done((bf16[1024,1024]{1,0:T(8,128)(2,1)S(1)}, bf16[1024,1024]{1,0:T(8,128)(2,1)}, u32[]{:S(2)}) %copy-start) | copy-done | bytes 2097176
  2.9 0.0 copy-start.1
  2.9 1.2 %copy-done.1 = bf16[4,128,1024]{2,1,0:T(8,128)(2,1)S(1)} copy-done((bf16[4,128,1024]{2,1,0:T(8,128)(2,1)S(1)}, bf16[4,128,1024]{2,1,0:T(8,128)(2,1)}, u32[]{:S(2)}) %copy-start.1) | copy-done | bytes 1048600
  4.1 0.0 copy-start.2
  4.1 1.2 %copy-done.2 = bf16[1024,512]{1,0:T(8,128)(2,1)S(1)} copy-done((bf16[1024,512]{1,0:T(8,128)(2,1)S(1)}, bf16[1024,512]{1,0:T(8,128)(2,1)}, u32[]{:S(2)}) %copy-start.2) | copy-done | bytes 1048600
  5.4 0.0 copy-start.3
  5.4 0.9 copy-done.3
  6.3 0.0 copy-start.4
  6.3 0.7 copy-done.4
  7.0 0.0 copy-start.5
  7.0 0.7 copy-done.5
  7.6 95.9 %shard_map.94 = (bf16[1,128,512]{2,1,0:T(8,128)(2,1)S(1)}, bf16[1024,1024]{1,0:T(8,128)(2,1)S(1)}, bf16[1024,512]{1,0:T(8,128)(2,1)S(1)}) custom-call(bf16[4,128,1024]{2,1,0:T(8,128)(2,1)S(1)} %copy-done.1, bf16[1024,1024]{1,0:T(8,128)(2,1)S(1)} %copy-done, bf16[1024,512]{1,0:T(8,128)(2,1)S(1)} %copy-done.2, s32[10,128]{1,0:T(8,128)S(1)} %bitcast.8, ...), custom_call_target="tpu_custom_call" | custom-call | tf_op jit(solution)/shard_map/pallas_call | solution.py:439
  103.5 2.6 %convert_multiply_fusion = f32[1024,1024]{1,0:T(8,128)} fusion(bf16[1024,1024]{1,0:T(8,128)(2,1)S(1)} %get-tuple-element.7), kind=kLoop, calls=%fused_computation | loop fusion | flops 2097152 | bytes 6291456 | tf_op jit(solution)/shard_map/mul | solution.py:454
  106.1 1.6 %convert_multiply_fusion.1 = f32[1024,512]{1,0:T(8,128)} fusion(bf16[1024,512]{1,0:T(8,128)(2,1)S(1)} %get-tuple-element.8), kind=kLoop, calls=%fused_computation.1 | loop fusion | flops 1048576 | bytes 3145728 | tf_op jit(solution)/shard_map/mul | solution.py:454
  107.7 0.7 copy.14
Async XLA Ops:
  1.3 1.6 %copy-start = (bf16[1024,1024]{1,0:T(8,128)(2,1)S(1)}, bf16[1024,1024]{1,0:T(8,128)(2,1)}, u32[]{:S(2)}) copy-start(bf16[1024,1024]{1,0:T(8,128)(2,1)} %w_one.1) | copy-start | bytes 6291460
  2.9 1.2 %copy-start.1 = (bf16[4,128,1024]{2,1,0:T(8,128)(2,1)S(1)}, bf16[4,128,1024]{2,1,0:T(8,128)(2,1)}, u32[]{:S(2)}) copy-start(bf16[4,128,1024]{2,1,0:T(8,128)(2,1)} %feats.1) | copy-start | bytes 3145732
  4.1 1.2 %copy-start.2 = (bf16[1024,512]{1,0:T(8,128)(2,1)S(1)}, bf16[1024,512]{1,0:T(8,128)(2,1)}, u32[]{:S(2)}) copy-start(bf16[1024,512]{1,0:T(8,128)(2,1)} %w_two.1) | copy-start | bytes 3145732
  5.4 0.9 copy-start.3
  6.3 0.7 copy-start.4
  7.0 0.7 copy-start.5

commit v3 on v2

--- a/solution.py
+++ b/solution.py
@@ -24,15 +24,16 @@
 
 def kernel(
     feat, nx, nz, kmax,
+    feats_hbm, w_one_hbm, w_two_hbm, nbr_hbm, deg_hbm, sends_hbm, grads_hbm,
+    out, one, two,
     feats, w_one, w_two, nbr, deg, sends, grads,
-    out, one, two,
     proj, projb, r1, q, qb, r2, cm, ct, sm, st, t1, t2, b1, b2, k0, k1, h0, h1,
     inv, dcs, dh, pself, dnl, joined, fx, ft, dp, g, rx, sx, rz, ts, u1, ub, u2, v, vx, vs, vz,
-    ssem, rsem,
+    ssem, rsem, lsem,
 ):
     ny = feat // 2
     parts = nx * nz
-    n = nbr.shape[1]
+    n = nbr.shape[2]
     w = grads.shape[1]
     cols = w_one.shape[0]
     fan = nbr.shape[0]
@@ -68,9 +69,20 @@
     for device in everyone:
         pl.semaphore_signal(barrier, inc=1, device_id=device, device_id_type=pl.DeviceIdType.MESH)
 
-    flat = feats[...].reshape(feat * n, cols)
+    def load(k, src, dst):
+        copy = pltpu.make_async_copy(src, dst, lsem.at[k])
+        copy.start()
+        return copy
+
+    first_loads = [load(0, w_one_hbm.at[:, w:], w_one.at[:, w:]), load(1, feats_hbm, feats)]
+    self_load = load(2, w_one_hbm.at[:, :w], w_one.at[:, :w])
+    later_loads = [
+        load(3, nbr_hbm, nbr), load(4, deg_hbm, deg), load(5, sends_hbm, sends),
+        load(6, grads_hbm, grads), load(7, w_two_hbm, w_two),
+    ]
 
     def project(h):
+        flat = feats[...].reshape(feat * n, cols)
         for t in range(w // TILE):
             acc = dot(flat, w_one[:, h * w + t * TILE : h * w + (t + 1) * TILE])
             for f in range(feat):
@@ -123,47 +135,51 @@
         moves = [send(outgoing.at[slot(p)], returned.at[slot(di)], (fi, p)) for p in dpeers]
         return terms[:n], moves
 
-    def block(low, f, h):
-        return dp.at[low, f, :, h * w : (h + 1) * w]
-
-    def pass_on(low, f, h, device):
-        return send(block(low, f, h), block(low, f, h), device)
+    def pass_on(low, f, k, device):
+        block = dp.at[low, f, :, k * TILE : (k + 1) * TILE]
+        return send(block, block, device)
 
     def y_source(o):
         return lax.rem(y - o + ny, ny) * 2 + c
 
-    def gather_start(h):
-        to_pair = pass_on(zlow, fi, h, pair)
-        to_y = [pass_on(zlow, fi, h, device) for device in ypeers]
-        return to_pair, to_y, [pass_on(zlow, fi, h, mate)]
-
-    def gather_y_first(h, to_pair, to_y, to_mate):
-        paired = [to_pair]
+    def gather_start(k):
+        to_pair = pass_on(zlow, fi, k, pair)
+        to_y = [pass_on(zlow, fi, k, device) for device in ypeers]
+        return [to_pair], to_y, [pass_on(zlow, fi, k, mate)]
+
+    def gather_forward(k, to_pair, to_y, to_mate):
+        if k % 2:
+            to_pair[0].wait_recv()
+            far = [pass_on(1 - zlow, fi, k, device) for device in ypeers]
+            to_mate.append(pass_on(1 - zlow, fi, k, mate))
+            return far, to_y, to_mate
         for o in range(1, ny):
             to_y[o - 1].wait_recv()
-            paired.append(pass_on(zlow, y_source(o), h, pair))
-            to_mate.append(pass_on(zlow, y_source(o), h, mate))
+            to_pair.append(pass_on(zlow, y_source(o), k, pair))
+            to_mate.append(pass_on(zlow, y_source(o), k, mate))
+        return to_pair, to_y, to_mate
+
+    def gather_end(k, later, to_y, to_mate):
+        if k % 2:
+            for low, moves in ((zlow, to_y), (1 - zlow, later)):
+                for o in range(1, ny):
+                    moves[o - 1].wait_recv()
+                    to_mate.append(pass_on(low, y_source(o), k, mate))
+            return to_mate
         for o in range(ny):
-            paired[o].wait_recv()
-            to_mate.append(pass_on(1 - zlow, y_source(o), h, mate))
+            later[o].wait_recv()
+            to_mate.append(pass_on(1 - zlow, y_source(o), k, mate))
         return to_mate
 
-    def gather_pair_first(h, to_pair, to_y, to_mate):
-        to_pair.wait_recv()
-        far = [pass_on(1 - zlow, fi, h, device) for device in ypeers]
-        to_mate.append(pass_on(1 - zlow, fi, h, mate))
-        for low, moves in ((zlow, to_y), (1 - zlow, far)):
-            for o in range(1, ny):
-                moves[o - 1].wait_recv()
-                to_mate.append(pass_on(low, y_source(o), h, mate))
-        return to_mate
-
+    for item in first_loads:
+        item.wait()
     project(1)
     pl.semaphore_wait(barrier, len(everyone))
     near_core = core_send(1)
     far_cols = pl.ds(pl.multiple_of((1 - zlow) * half_cols, 128), half_cols)
     near_cols = pl.ds(pl.multiple_of(zlow * half_cols, 128), half_cols)
     features_move = send(feats.at[:, :, far_cols], fx, pair)
+    self_load.wait()
     project(0)
     self_core = core_send(0)
     near_core.wait_recv()
@@ -171,6 +187,8 @@
     self_core.wait_recv()
     self_y = y_send(0)
 
+    for item in later_loads:
+        item.wait()
     eye = lax.broadcasted_iota(jnp.int32, (n, n), 0) == lax.broadcasted_iota(jnp.int32, (n, n), 1)
     inv[...] = 1.0 / jnp.sum(jnp.where(eye, deg[...].astype(F32), 0.0), axis=1, keepdims=True)
     entry = lax.broadcasted_iota(jnp.int32, (n + parts * SLOT, n), 0)
@@ -181,7 +199,7 @@
     )
     counts = jnp.zeros(code.shape, F32)
     for s in range(fan):
-        used = jnp.where(s < deg[...], nbr[s : s + 1], -1)
+        used = jnp.where(s < deg[...], nbr[s], -1)
         counts = counts + jnp.where(used == code, 1.0, 0.0)
     ct[...] = counts.astype(BF)
     cm[...] = counts.T.astype(BF)
@@ -212,18 +230,25 @@
     sig = 1.0 / (1.0 + jnp.exp(-pre))
     d_pre = dh[...] * sig * (1.0 + pre * (1.0 - sig))
     dp[zlow, fi, :, :w] = d_pre.astype(BF)
+    chunks = 2 * w // TILE
+    half = chunks // 2
+    gathers = {}
     near_local, back_pre = trade_back(d_pre, k1, h1)
     dnl[...] = near_local
-    gather0 = gather_start(0)
+    for k in range(half):
+        gathers[k] = gather_start(k)
     hidden = (pre * sig).astype(BF)
     joined[:, :w] = hidden
     rows_hidden = trade_rows(hidden, b2, t2)
 
+    features_move.wait_recv()
+    ft[1 - zlow] = fx[...].reshape(feat * n, half_cols).T
     wait(back_pre)
     dp[zlow, fi, :, w:] = (dnl[...] + dot(st[...], h1[...])).astype(BF)
-    gather1 = gather_start(1)
-    features_move.wait_recv()
-    ft[1 - zlow] = fx[...].reshape(feat * n, half_cols).T
+    for k in range(half, chunks):
+        gathers[k] = gather_start(k)
+    for k in range(half):
+        gathers[k] = gather_forward(k, *gathers[k])
 
     wait(rows_hidden)
     agg = dot(cm[...], t2[...]) * inv[...]
@@ -236,8 +261,10 @@
         ts[f % 2, (f // 2) * span : (f // 2 + 1) * span] = two_part[f * span : (f + 1) * span]
     two_core = send(ts.at[1 - c], u1, mate)
 
-    arrived0 = gather_y_first(0, *gather0)
-    arrived1 = gather_pair_first(1, *gather1)
+    for k in range(half, chunks):
+        gathers[k] = gather_forward(k, *gathers[k])
+    for k in range(half):
+        gathers[k] = gather_end(k, *gathers[k])
 
     rows_x = half_cols // nx
     rows_z = rows_x // (nz // 2)
@@ -368,16 +395,16 @@
             across.append(send(piece, piece, mate))
         return across
 
-    chunks = 2 * w // TILE
-    half = chunks // 2
     moves = {}
     two_moves = two_y()
-    wait(arrived0)
     for k in range(half):
+        wait(gathers[k])
         moves[k] = chunk(k)
+    for k in range(half, chunks):
+        gathers[k] = gather_end(k, *gathers[k])
     two_moves = two_x(two_moves)
-    wait(arrived1)
     for k in range(half, chunks):
+        wait(gathers[k])
         moves[k] = chunk(k)
     stages = [z_scatter, z_gather, first_gather, last_gather]
     two_stages = [two_z, two_zg, two_xg]
@@ -400,6 +427,21 @@
         copy.wait_send()
 
 
+def finish(scale, out, one, two, out_hbm, one_hbm, two_hbm, one_wide, two_wide, sem):
+    copies = [pltpu.make_async_copy(out, out_hbm, sem.at[0])]
+    copies[0].start()
+    for narrow, wide, target in ((one, one_wide, one_hbm), (two, two_wide, two_hbm)):
+        rows = narrow.shape[0] // 4
+        for k in range(4):
+            part = slice(k * rows, (k + 1) * rows)
+            wide[part] = narrow[part].astype(F32) * scale
+            copy = pltpu.make_async_copy(wide.at[part], target.at[part], sem.at[len(copies)])
+            copy.start()
+            copies.append(copy)
+    for copy in copies:
+        copy.wait()
+
+
 def on_device(nx, nz, features, w_one, w_two, neighbor, degree, send_rows, grad_out):
     feat, n, cols = features.shape
     w = w_two.shape[1]
@@ -414,12 +456,15 @@
     lanes_x = w // nx
     chunks = 2 * w // TILE
     n_copies = (
-        3 + 2 * (ny - 1) + 4 * (parts - 1) + 2 * (2 + 2 * ny) + 4 * ny
-        + chunks * (4 * nx + nz)
+        3 + 2 * (ny - 1) + 4 * (parts - 1)
+        + chunks * (4 * ny + 2 + 4 * nx + nz)
         + 2 + 4 * ny + 2 * (nx + nz)
     )
     vm = pltpu.VMEM
     scratch = [
+        vm(features.shape, BF), vm(w_one.shape, BF), vm(w_two.shape, BF),
+        vm((neighbor.shape[2], 1, n), jnp.int32), vm((1, n), jnp.int32),
+        vm((parts, kmax), jnp.int32), vm((n, w), BF),
         vm((2, 2, ny * n, w), F32), vm((2, 2, ny * n, w), BF), vm((2, ny * n, w), BF),
         vm((2, n, w), F32), vm((2, ny, n, w), BF), vm((2, ny - 1, n, w), BF),
         vm((n, table), BF), vm((table, n), BF), vm((edge, n), BF), vm((n, edge), BF),
@@ -434,8 +479,10 @@
         vm((ny - 1, span, w), BF), vm((nx, span, lanes_x), BF), vm((nx - 1, span, lanes_x), BF),
         vm((span, lanes_x), BF), vm((nz - 1, span // nz, lanes_x), BF),
         pltpu.SemaphoreType.DMA((n_copies,)), pltpu.SemaphoreType.DMA((n_copies,)),
+        pltpu.SemaphoreType.DMA((8,)),
     ]
     spec = pl.BlockSpec(memory_space=pltpu.VMEM)
+    hbm = pl.BlockSpec(memory_space=pltpu.HBM)
     out, one_sum, two_sum = pl.pallas_call(
         functools.partial(kernel, feat, nx, nz, kmax),
         out_shape=(
@@ -443,15 +490,35 @@
             jax.ShapeDtypeStruct((cols, 2 * w), BF),
             jax.ShapeDtypeStruct((2 * w, w), BF),
         ),
-        in_specs=[spec] * 7,
+        in_specs=[hbm] * 7,
         out_specs=(spec, spec, spec),
         scratch_shapes=scratch,
         compiler_params=pltpu.CompilerParams(
             collective_id=0, has_side_effects=True, vmem_limit_bytes=40 * 1024 * 1024
         ),
-    )(features, w_one, w_two, neighbor[0].T, degree, send_rows[0], grad_out[0])
+    )(*(
+        pltpu.with_memory_space_constraint(operand, pltpu.HBM)
+        for operand in (
+            features, w_one, w_two, jnp.transpose(neighbor, (2, 0, 1)), degree, send_rows[0],
+            grad_out[0],
+        )
+    ))
     scale = 1.0 / math.sqrt(feat * n * parts)
-    return out, one_sum.astype(F32) * scale, two_sum.astype(F32) * scale
+    wide = (
+        jax.ShapeDtypeStruct(out.shape, BF),
+        jax.ShapeDtypeStruct(one_sum.shape, F32),
+        jax.ShapeDtypeStruct(two_sum.shape, F32),
+    )
+    return pl.pallas_call(
+        functools.partial(finish, scale),
+        out_shape=wide,
+        in_specs=[spec] * 3,
+        out_specs=(hbm, hbm, hbm),
+        scratch_shapes=[
+            vm(one_sum.shape, F32), vm(two_sum.shape, F32), pltpu.SemaphoreType.DMA((9,)),
+        ],
+        compiler_params=pltpu.CompilerParams(vmem_limit_bytes=16 * 1024 * 1024),
+    )(out, one_sum, two_sum)
 
 
 def solution(mesh):

time: 109 us -> 97.8 us (0.90)
  local copies, waits for them, and re-layouts: 7.63 us -> 0 us
  other arithmetic: 4.22 us -> 0 us
  Pallas kernels: 95.9 us -> 97.1 us
    unnamed x14 -> x0, local copies, waits for them, and re-layouts: 7.63 us -> none
    mul x2 -> x0, other arithmetic: 4.22 us -> none  [on_device(): return (out, one_sum.astype(F32) * scale, two_sum.astype(F32) * scale)]
    pallas_call x0 -> x1, Pallas kernels: none -> 2.8 us  [on_device(): pl.pallas_call(functools.partial(finish, scale), out_shape=wide, in_specs...]
    pallas_call x1, Pallas kernels: 95.9 us -> 94.3 us  [on_device(): pl.pallas_call(functools.partial(kernel, feat, nx, nz, kmax), out_shape=(...]
where the time goes in v3:
time: 97.8 us; the launch traced here: 97.7 us
  Pallas kernels  97.1 us (99%)
    pallas_call x1, Pallas kernels, on_device(): pl.pallas_call(functools.partial(kernel, feat, nx, nz, kmax), out_shape=(...  94.3 us
    pallas_call x1, Pallas kernels, on_device(): pl.pallas_call(functools.partial(finish, scale), out_shape=wide, in_specs...  2.8 us

profile of v3, /device:TPU:0, one launch (start us, length us, event | category | flops | bytes accessed | tf_op | source)
XLA Modules:
  0.0 97.7 jit_solution(14258712785927394088)
XLA Ops:
  0.6 94.3 %shard_map.94 = (bf16[1,128,512]{2,1,0:T(8,128)(2,1)S(1)}, bf16[1024,1024]{1,0:T(8,128)(2,1)S(1)}, bf16[1024,512]{1,0:T(8,128)(2,1)S(1)}) custom-call(bf16[4,128,1024]{2,1,0:T(8,128)(2,1)} %feats_hbm.1, bf16[1024,1024]{1,0:T(8,128)(2,1)} %w_one_hbm.1, bf16[1024,512]{1,0:T(8,128)(2,1)} %w_two_hbm.1, s32[10,1,128]{2,1,0:T(1,128)} %bitcast.4, ...), custom_call_target="tpu_custom_call" | custom-call | tf_op jit(solution)/shard_map/pallas_call | solution.py:486
  94.9 2.8 %shard_map.95 = (bf16[1,128,512]{2,1,0:T(8,128)(2,1)}, f32[1024,1024]{1,0:T(8,128)}, f32[1024,512]{1,0:T(8,128)}) custom-call(bf16[1,128,512]{2,1,0:T(8,128)(2,1)S(1)} %get-tuple-element.6.out, bf16[1024,1024]{1,0:T(8,128)(2,1)S(1)} %get-tuple-element.7.one, bf16[1024,512]{1,0:T(8,128)(2,1)S(1)} %get-tuple-element.8.two), custom_call_target="tpu_custom_call" | custom-call | tf_op jit(solution)/shard_map/pallas_call | solution.py:512

commit v4 on v3

--- a/solution.py
+++ b/solution.py
@@ -28,7 +28,7 @@
     out, one, two,
     feats, w_one, w_two, nbr, deg, sends, grads,
     proj, projb, r1, q, qb, r2, cm, ct, sm, st, t1, t2, b1, b2, k0, k1, h0, h1,
-    inv, dcs, dh, pself, dnl, joined, fx, ft, dp, g, rx, sx, rz, ts, u1, ub, u2, v, vx, vs, vz,
+    inv, dcs, dh, pself, dnl, joined, fx, ft, dp, g, rx, rz, ts, u1, ub, u2, v, vx, vs, vz,
     ssem, rsem, lsem,
 ):
     ny = feat // 2
@@ -171,14 +171,14 @@
             to_mate.append(pass_on(1 - zlow, y_source(o), k, mate))
         return to_mate
 
-    for item in first_loads:
-        item.wait()
-    project(1)
+    first_loads[1].wait()
     pl.semaphore_wait(barrier, len(everyone))
-    near_core = core_send(1)
     far_cols = pl.ds(pl.multiple_of((1 - zlow) * half_cols, 128), half_cols)
     near_cols = pl.ds(pl.multiple_of(zlow * half_cols, 128), half_cols)
     features_move = send(feats.at[:, :, far_cols], fx, pair)
+    first_loads[0].wait()
+    project(1)
+    near_core = core_send(1)
     self_load.wait()
     project(0)
     self_core = core_send(0)
@@ -217,10 +217,10 @@
     dcs[...] = dcat[:, :w]
     local, back_agg = trade_back(dcat[:, w:], k0, h0)
     dcs[...] += local
-    ft[zlow] = feats[:, :, near_cols].reshape(feat * n, half_cols).T
 
     wait(near_y)
     rows_near = trade_rows(owned(1).astype(BF), b1, t1)
+    ft[zlow] = feats[:, :, near_cols].reshape(feat * n, half_cols).T
     wait(self_y)
     pself[...] = owned(0)
     wait(back_agg)
@@ -267,7 +267,6 @@
         gathers[k] = gather_end(k, *gathers[k])
 
     rows_x = half_cols // nx
-    rows_z = rows_x // (nz // 2)
 
     def lanes_of(k):
         return slice(k * TILE, (k + 1) * TILE)
@@ -284,36 +283,27 @@
             for o, t in enumerate(xpeers)
         ]
 
-    def z_scatter(k, moves):
+    def z_exchange(k, moves):
         wait(moves)
         lanes = lanes_of(k)
         total = g[pl.ds(pl.multiple_of(x * rows_x, SLOT), rows_x), lanes].astype(F32)
         for o in range(nx - 1):
             total = total + rx[o, :, lanes].astype(F32)
-        sx[:, lanes] = total.astype(BF)
-        return [
-            send(sx.at[pl.ds(pl.multiple_of((t // 2) * rows_z, SLOT), rows_z), lanes],
-                 rz.at[o, :, lanes], (fi, t * nx + x))
-            for o, t in enumerate(zpeers)
-        ]
+        rz[zhigh, :, lanes] = total.astype(BF)
+        part = rz.at[zhigh, :, lanes]
+        return [send(part, part, (fi, t * nx + x)) for t in zpeers]
 
     def piece(k, low, at):
         return one.at[pl.ds(pl.multiple_of(low * half_cols + at * rows_x, SLOT), rows_x), lanes_of(k)]
 
-    def z_gather(k, moves):
+    def first_gather(k, moves):
         wait(moves)
         lanes = lanes_of(k)
-        total = sx[pl.ds(pl.multiple_of(zhigh * rows_z, SLOT), rows_z), lanes].astype(F32)
-        for o in range(nz // 2 - 1):
+        total = rz[0, :, lanes].astype(F32)
+        for o in range(1, nz // 2):
             total = total + rz[o, :, lanes].astype(F32)
-        mine = pl.ds(
-            pl.multiple_of(zlow * half_cols + x * rows_x + zhigh * rows_z, SLOT), rows_z
-        )
-        one[mine, lanes] = total.astype(BF)
-        return [send(one.at[mine, lanes], one.at[mine, lanes], (fi, t * nx + x)) for t in zpeers]
-
-    def first_gather(k, moves):
-        wait(moves)
+        rows = pl.ds(pl.multiple_of(zlow * half_cols + x * rows_x, SLOT), rows_x)
+        one[rows, lanes] = total.astype(BF)
         mine = piece(k, zlow, x)
         to_x = [send(mine, mine, (fi, z * nx + t)) for t in xpeers]
         return to_x, send(mine, mine, pair)
@@ -396,6 +386,7 @@
         return across
 
     moves = {}
+    marks = [len(copies)]
     two_moves = two_y()
     for k in range(half):
         wait(gathers[k])
@@ -406,9 +397,11 @@
     for k in range(half, chunks):
         wait(gathers[k])
         moves[k] = chunk(k)
-    stages = [z_scatter, z_gather, first_gather, last_gather]
+    stages = [z_exchange, first_gather, last_gather]
+    drained = 0
     two_stages = [two_z, two_zg, two_xg]
     for step in range(chunks + len(stages) - 1):
+        marks.append(len(copies))
         for s in reversed(range(len(stages))):
             k = step - s
             if 0 <= k < chunks:
@@ -419,11 +412,15 @@
             two_moves, two_mate = two_yg(two_moves)
         elif step == len(two_stages) + 1:
             two_moves = two_across(two_moves)
+        settled = marks[max(step - 1, 0)]
+        for copy in copies[drained:settled]:
+            copy.wait_send()
+        drained = settled
     for k in range(chunks):
         wait(moves[k])
     wait(two_moves)
     two_mate.wait_recv()
-    for copy in copies:
+    for copy in copies[drained:]:
         copy.wait_send()
 
 
@@ -451,7 +448,6 @@
     edge = parts * SLOT
     half_cols = cols // 2
     rows_x = half_cols // nx
-    rows_z = rows_x // (nz // 2)
     span = 2 * w // feat
     lanes_x = w // nx
     chunks = 2 * w // TILE
@@ -473,8 +469,8 @@
         vm((n, 1), F32), vm((n, w), F32), vm((n, w), F32), vm((n, w), F32), vm((n, w), F32),
         vm((n, 2 * w), BF), vm((feat, n, half_cols), BF), vm((2, half_cols, feat * n), BF),
         vm((2, feat, n, 2 * w), BF),
-        vm((half_cols, 2 * w), BF), vm((nx - 1, rows_x, 2 * w), BF), vm((rows_x, 2 * w), BF),
-        vm((nz // 2 - 1, rows_z, 2 * w), BF),
+        vm((half_cols, 2 * w), BF), vm((nx - 1, rows_x, 2 * w), BF),
+        vm((nz // 2, rows_x, 2 * w), BF),
         vm((2, ny * span, w), BF), vm((ny * span, w), BF), vm((ny * span, w), BF),
         vm((ny - 1, span, w), BF), vm((nx, span, lanes_x), BF), vm((nx - 1, span, lanes_x), BF),
         vm((span, lanes_x), BF), vm((nz - 1, span // nz, lanes_x), BF),

time: 97.8 us -> 96.1 us (0.983)
  Pallas kernels: 97.1 us -> 95.3 us
    pallas_call x1, Pallas kernels: 94.3 us -> 92.5 us  [on_device(): pl.pallas_call(functools.partial(kernel, feat, nx, nz, kmax), out_shape=(...]
where the time goes in v4:
time: 96.1 us; the launch traced here: 96 us
  Pallas kernels  95.3 us (99%)
    pallas_call x1, Pallas kernels, on_device(): pl.pallas_call(functools.partial(kernel, feat, nx, nz, kmax), out_shape=(...  92.5 us
    pallas_call x1, Pallas kernels, on_device(): pl.pallas_call(functools.partial(finish, scale), out_shape=wide, in_specs...  2.8 us

profile of v4, /device:TPU:0, one launch (start us, length us, event | category | flops | bytes accessed | tf_op | source)
XLA Modules:
  0.0 96.0 jit_solution(11263328837601942799)
XLA Ops:
  0.6 92.5 %shard_map.94 = (bf16[1,128,512]{2,1,0:T(8,128)(2,1)S(1)}, bf16[1024,1024]{1,0:T(8,128)(2,1)S(1)}, bf16[1024,512]{1,0:T(8,128)(2,1)S(1)}) custom-call(bf16[4,128,1024]{2,1,0:T(8,128)(2,1)} %feats_hbm.1, bf16[1024,1024]{1,0:T(8,128)(2,1)} %w_one_hbm.1, bf16[1024,512]{1,0:T(8,128)(2,1)} %w_two_hbm.1, s32[10,1,128]{2,1,0:T(1,128)} %bitcast.4, ...), custom_call_target="tpu_custom_call" | custom-call | tf_op jit(solution)/shard_map/pallas_call | solution.py:482
  93.2 2.8 %shard_map.95 = (bf16[1,128,512]{2,1,0:T(8,128)(2,1)}, f32[1024,1024]{1,0:T(8,128)}, f32[1024,512]{1,0:T(8,128)}) custom-call(bf16[1,128,512]{2,1,0:T(8,128)(2,1)S(1)} %get-tuple-element.6.out, bf16[1024,1024]{1,0:T(8,128)(2,1)S(1)} %get-tuple-element.7.one, bf16[1024,512]{1,0:T(8,128)(2,1)S(1)} %get-tuple-element.8.two), custom_call_target="tpu_custom_call" | custom-call | tf_op jit(solution)/shard_map/pallas_call | solution.py:508

commit v5 on v4

--- a/solution.py
+++ b/solution.py
@@ -136,7 +136,7 @@
         return terms[:n], moves
 
     def pass_on(low, f, k, device):
-        block = dp.at[low, f, :, k * TILE : (k + 1) * TILE]
+        block = dp.at[low, f, k]
         return send(block, block, device)
 
     def y_source(o):
@@ -229,9 +229,10 @@
     pre = pself[...] + dot(cm[...], t1[...]) * inv[...]
     sig = 1.0 / (1.0 + jnp.exp(-pre))
     d_pre = dh[...] * sig * (1.0 + pre * (1.0 - sig))
-    dp[zlow, fi, :, :w] = d_pre.astype(BF)
     chunks = 2 * w // TILE
     half = chunks // 2
+    for k in range(half):
+        dp[zlow, fi, k] = d_pre[:, k * TILE : (k + 1) * TILE].astype(BF)
     gathers = {}
     near_local, back_pre = trade_back(d_pre, k1, h1)
     dnl[...] = near_local
@@ -244,7 +245,9 @@
     features_move.wait_recv()
     ft[1 - zlow] = fx[...].reshape(feat * n, half_cols).T
     wait(back_pre)
-    dp[zlow, fi, :, w:] = (dnl[...] + dot(st[...], h1[...])).astype(BF)
+    d_near = (dnl[...] + dot(st[...], h1[...])).astype(BF)
+    for k in range(half):
+        dp[zlow, fi, half + k] = d_near[:, k * TILE : (k + 1) * TILE]
     for k in range(half, chunks):
         gathers[k] = gather_start(k)
     for k in range(half):
@@ -268,43 +271,36 @@
 
     rows_x = half_cols // nx
 
-    def lanes_of(k):
-        return slice(k * TILE, (k + 1) * TILE)
-
     def chunk(k):
-        lanes = lanes_of(k)
-        g[:, lanes] = (
-            dot(ft[0], dp[0, :, :, lanes].reshape(feat * n, TILE))
-            + dot(ft[1], dp[1, :, :, lanes].reshape(feat * n, TILE))
+        g[k] = (
+            dot(ft[0], dp[0, :, k].reshape(feat * n, TILE))
+            + dot(ft[1], dp[1, :, k].reshape(feat * n, TILE))
         ).astype(BF)
         return [
-            send(g.at[pl.ds(pl.multiple_of(t * rows_x, SLOT), rows_x), lanes],
-                 rx.at[o, :, lanes], (fi, z * nx + t))
+            send(g.at[k, pl.ds(pl.multiple_of(t * rows_x, SLOT), rows_x)], rx.at[o, k],
+                 (fi, z * nx + t))
             for o, t in enumerate(xpeers)
         ]
 
     def z_exchange(k, moves):
         wait(moves)
-        lanes = lanes_of(k)
-        total = g[pl.ds(pl.multiple_of(x * rows_x, SLOT), rows_x), lanes].astype(F32)
+        total = g[k, pl.ds(pl.multiple_of(x * rows_x, SLOT), rows_x)].astype(F32)
         for o in range(nx - 1):
-            total = total + rx[o, :, lanes].astype(F32)
-        rz[zhigh, :, lanes] = total.astype(BF)
-        part = rz.at[zhigh, :, lanes]
+            total = total + rx[o, k].astype(F32)
+        rz[zhigh, k] = total.astype(BF)
+        part = rz.at[zhigh, k]
         return [send(part, part, (fi, t * nx + x)) for t in zpeers]
 
     def piece(k, low, at):
-        return one.at[pl.ds(pl.multiple_of(low * half_cols + at * rows_x, SLOT), rows_x), lanes_of(k)]
+        return one.at[k, pl.ds(pl.multiple_of(low * half_cols + at * rows_x, SLOT), rows_x)]
 
     def first_gather(k, moves):
         wait(moves)
-        lanes = lanes_of(k)
-        total = rz[0, :, lanes].astype(F32)
+        total = rz[0, k].astype(F32)
         for o in range(1, nz // 2):
-            total = total + rz[o, :, lanes].astype(F32)
-        rows = pl.ds(pl.multiple_of(zlow * half_cols + x * rows_x, SLOT), rows_x)
-        one[rows, lanes] = total.astype(BF)
+            total = total + rz[o, k].astype(F32)
         mine = piece(k, zlow, x)
+        mine[...] = total.astype(BF)
         to_x = [send(mine, mine, (fi, z * nx + t)) for t in xpeers]
         return to_x, send(mine, mine, pair)
 
@@ -387,32 +383,33 @@
 
     moves = {}
     marks = [len(copies)]
+    drained = 0
     two_moves = two_y()
     for k in range(half):
         wait(gathers[k])
         moves[k] = chunk(k)
     for k in range(half, chunks):
         gathers[k] = gather_end(k, *gathers[k])
-    two_moves = two_x(two_moves)
     for k in range(half, chunks):
         wait(gathers[k])
         moves[k] = chunk(k)
-    stages = [z_exchange, first_gather, last_gather]
-    drained = 0
-    two_stages = [two_z, two_zg, two_xg]
-    for step in range(chunks + len(stages) - 1):
+        moves[k - half] = z_exchange(k - half, moves[k - half])
+    two_stages = [two_x, two_z, two_zg, two_xg]
+    for step in range(1, chunks + 3):
         marks.append(len(copies))
-        for s in reversed(range(len(stages))):
-            k = step - s
-            if 0 <= k < chunks:
-                moves[k] = stages[s](k, moves[k])
-        if step < len(two_stages):
-            two_moves = two_stages[step](two_moves)
-        elif step == len(two_stages):
+        if half <= step < chunks:
+            moves[step] = z_exchange(step, moves[step])
+        if step >= 3:
+            moves[step - 3] = last_gather(step - 3, moves[step - 3])
+        if step <= chunks:
+            moves[step - 1] = first_gather(step - 1, moves[step - 1])
+        if step <= len(two_stages):
+            two_moves = two_stages[step - 1](two_moves)
+        elif step == len(two_stages) + 1:
             two_moves, two_mate = two_yg(two_moves)
-        elif step == len(two_stages) + 1:
+        elif step == len(two_stages) + 2:
             two_moves = two_across(two_moves)
-        settled = marks[max(step - 1, 0)]
+        settled = marks[max(step - 2, 0)]
         for copy in copies[drained:settled]:
             copy.wait_send()
         drained = settled
@@ -427,11 +424,16 @@
 def finish(scale, out, one, two, out_hbm, one_hbm, two_hbm, one_wide, two_wide, sem):
     copies = [pltpu.make_async_copy(out, out_hbm, sem.at[0])]
     copies[0].start()
-    for narrow, wide, target in ((one, one_wide, one_hbm), (two, two_wide, two_hbm)):
-        rows = narrow.shape[0] // 4
+    for wide, target in ((one_wide, one_hbm), (two_wide, two_hbm)):
+        rows = wide.shape[0] // 4
         for k in range(4):
             part = slice(k * rows, (k + 1) * rows)
-            wide[part] = narrow[part].astype(F32) * scale
+            if wide is one_wide:
+                for lane in range(one.shape[0]):
+                    lanes = slice(lane * TILE, (lane + 1) * TILE)
+                    wide[part, lanes] = one[lane, part].astype(F32) * scale
+            else:
+                wide[part] = two[part].astype(F32) * scale
             copy = pltpu.make_async_copy(wide.at[part], target.at[part], sem.at[len(copies)])
             copy.start()
             copies.append(copy)
@@ -468,9 +470,9 @@
         vm((edge, w), BF), vm((edge, w), BF), vm((edge, w), BF), vm((edge, w), BF),
         vm((n, 1), F32), vm((n, w), F32), vm((n, w), F32), vm((n, w), F32), vm((n, w), F32),
         vm((n, 2 * w), BF), vm((feat, n, half_cols), BF), vm((2, half_cols, feat * n), BF),
-        vm((2, feat, n, 2 * w), BF),
-        vm((half_cols, 2 * w), BF), vm((nx - 1, rows_x, 2 * w), BF),
-        vm((nz // 2, rows_x, 2 * w), BF),
+        vm((2, feat, chunks, n, TILE), BF),
+        vm((chunks, half_cols, TILE), BF), vm((nx - 1, chunks, rows_x, TILE), BF),
+        vm((nz // 2, chunks, rows_x, TILE), BF),
         vm((2, ny * span, w), BF), vm((ny * span, w), BF), vm((ny * span, w), BF),
         vm((ny - 1, span, w), BF), vm((nx, span, lanes_x), BF), vm((nx - 1, span, lanes_x), BF),
         vm((span, lanes_x), BF), vm((nz - 1, span // nz, lanes_x), BF),
@@ -483,7 +485,7 @@
         functools.partial(kernel, feat, nx, nz, kmax),
         out_shape=(
             jax.ShapeDtypeStruct((1, n, w), BF),
-            jax.ShapeDtypeStruct((cols, 2 * w), BF),
+            jax.ShapeDtypeStruct((chunks, cols, TILE), BF),
             jax.ShapeDtypeStruct((2 * w, w), BF),
         ),
         in_specs=[hbm] * 7,
@@ -502,7 +504,7 @@
     scale = 1.0 / math.sqrt(feat * n * parts)
     wide = (
         jax.ShapeDtypeStruct(out.shape, BF),
-        jax.ShapeDtypeStruct(one_sum.shape, F32),
+        jax.ShapeDtypeStruct((cols, 2 * w), F32),
         jax.ShapeDtypeStruct(two_sum.shape, F32),
     )
     return pl.pallas_call(
@@ -511,7 +513,7 @@
         in_specs=[spec] * 3,
         out_specs=(hbm, hbm, hbm),
         scratch_shapes=[
-            vm(one_sum.shape, F32), vm(two_sum.shape, F32), pltpu.SemaphoreType.DMA((9,)),
+            vm((cols, 2 * w), F32), vm(two_sum.shape, F32), pltpu.SemaphoreType.DMA((9,)),
         ],
         compiler_params=pltpu.CompilerParams(vmem_limit_bytes=16 * 1024 * 1024),
     )(out, one_sum, two_sum)

time: 96.1 us -> 94.6 us (0.984)
  Pallas kernels: 95.3 us -> 93.8 us
    pallas_call x1, Pallas kernels: 92.5 us -> 91 us  [on_device(): pl.pallas_call(functools.partial(kernel, feat, nx, nz, kmax), out_shape=(...]
where the time goes in v5:
time: 94.6 us; the launch traced here: 94.4 us
  Pallas kernels  93.8 us (99%)
    pallas_call x1, Pallas kernels, on_device(): pl.pallas_call(functools.partial(kernel, feat, nx, nz, kmax), out_shape=(...  91 us
    pallas_call x1, Pallas kernels, on_device(): pl.pallas_call(functools.partial(finish, scale), out_shape=wide, in_specs...  2.8 us

profile of v5, /device:TPU:0, one launch (start us, length us, event | category | flops | bytes accessed | tf_op | source)
XLA Modules:
  0.0 94.4 jit_solution(4669619798761386834)
XLA Ops:
  0.6 91.0 %shard_map.94 = (bf16[1,128,512]{2,1,0:T(8,128)(2,1)S(1)}, bf16[4,1024,256]{2,1,0:T(8,128)(2,1)S(1)}, bf16[1024,512]{1,0:T(8,128)(2,1)S(1)}) custom-call(bf16[4,128,1024]{2,1,0:T(8,128)(2,1)} %feats_hbm.1, bf16[1024,1024]{1,0:T(8,128)(2,1)} %w_one_hbm.1, bf16[1024,512]{1,0:T(8,128)(2,1)} %w_two_hbm.1, s32[10,1,128]{2,1,0:T(1,128)} %bitcast.4, ...), custom_call_target="tpu_custom_call" | custom-call | tf_op jit(solution)/shard_map/pallas_call | solution.py:484
  91.6 2.8 %shard_map.95 = (bf16[1,128,512]{2,1,0:T(8,128)(2,1)}, f32[1024,1024]{1,0:T(8,128)}, f32[1024,512]{1,0:T(8,128)}) custom-call(bf16[1,128,512]{2,1,0:T(8,128)(2,1)S(1)} %get-tuple-element.6.out, bf16[4,1024,256]{2,1,0:T(8,128)(2,1)S(1)} %get-tuple-element.7.one, bf16[1024,512]{1,0:T(8,128)(2,1)S(1)} %get-tuple-element.8.two), custom_call_target="tpu_custom_call" | custom-call | tf_op jit(solution)/shard_map/pallas_call | solution.py:510

commit v6 on v5

--- a/solution.py
+++ b/solution.py
@@ -175,7 +175,10 @@
     pl.semaphore_wait(barrier, len(everyone))
     far_cols = pl.ds(pl.multiple_of((1 - zlow) * half_cols, 128), half_cols)
     near_cols = pl.ds(pl.multiple_of(zlow * half_cols, 128), half_cols)
-    features_move = send(feats.at[:, :, far_cols], fx, pair)
+    def send_features(f):
+        return send(feats.at[f, :, far_cols], fx.at[f], pair)
+
+    features_moves = [send_features(f) for f in range(feat // 2)]
     first_loads[0].wait()
     project(1)
     near_core = core_send(1)
@@ -195,7 +198,7 @@
     extra = entry - n
     code = jnp.where(
         entry < n, entry,
-        jnp.where(extra % SLOT < kmax, n + (extra // SLOT) * kmax + extra % SLOT, -2),
+        jnp.where((extra & 15) < kmax, n + (extra >> 4) * kmax + (extra & 15), -2),
     )
     counts = jnp.zeros(code.shape, F32)
     for s in range(fan):
@@ -204,10 +207,10 @@
     ct[...] = counts.astype(BF)
     cm[...] = counts.T.astype(BF)
     edge = (parts * SLOT, parts)
-    owner = lax.broadcasted_iota(jnp.int32, edge, 0) // SLOT == lax.broadcasted_iota(jnp.int32, edge, 1)
+    owner = lax.broadcasted_iota(jnp.int32, edge, 0) >> 4 == lax.broadcasted_iota(jnp.int32, edge, 1)
     spread_rows = dot(jnp.where(owner, 1.0, 0.0).astype(BF), sends[...].astype(F32).astype(BF))
     place = (parts * SLOT, kmax)
-    here = lax.broadcasted_iota(jnp.int32, place, 0) % SLOT == lax.broadcasted_iota(jnp.int32, place, 1)
+    here = lax.broadcasted_iota(jnp.int32, place, 0) & 15 == lax.broadcasted_iota(jnp.int32, place, 1)
     chosen = jnp.sum(jnp.where(here, spread_rows + 1.0, 0.0), axis=1, keepdims=True) - 1.0
     lane = lax.broadcasted_iota(jnp.int32, (parts * SLOT, n), 1).astype(F32)
     picks = jnp.where(chosen == lane, 1.0, 0.0)
@@ -220,6 +223,7 @@
 
     wait(near_y)
     rows_near = trade_rows(owned(1).astype(BF), b1, t1)
+    features_moves += [send_features(f) for f in range(feat // 2, feat)]
     ft[zlow] = feats[:, :, near_cols].reshape(feat * n, half_cols).T
     wait(self_y)
     pself[...] = owned(0)
@@ -242,7 +246,7 @@
     joined[:, :w] = hidden
     rows_hidden = trade_rows(hidden, b2, t2)
 
-    features_move.wait_recv()
+    wait(features_moves)
     ft[1 - zlow] = fx[...].reshape(feat * n, half_cols).T
     wait(back_pre)
     d_near = (dnl[...] + dot(st[...], h1[...])).astype(BF)
@@ -252,17 +256,6 @@
         gathers[k] = gather_start(k)
     for k in range(half):
         gathers[k] = gather_forward(k, *gathers[k])
-
-    wait(rows_hidden)
-    agg = dot(cm[...], t2[...]) * inv[...]
-    joined[:, w:] = agg.astype(BF)
-    both = joined[...]
-    out[0] = dot(both, w_two[...]).astype(BF)
-    span = two.shape[0] // feat
-    two_part = dot(both.T, grads[...]).astype(BF)
-    for f in range(feat):
-        ts[f % 2, (f // 2) * span : (f // 2 + 1) * span] = two_part[f * span : (f + 1) * span]
-    two_core = send(ts.at[1 - c], u1, mate)
 
     for k in range(half, chunks):
         gathers[k] = gather_forward(k, *gathers[k])
@@ -318,12 +311,24 @@
             rest.append(send(got, got, pair))
         return [to_pair] + rest
 
+    span = two.shape[0] // feat
     lanes_x = w // nx
     span_z = span // nz
     allz = [lax.rem(z + o, nz) for o in range(1, nz)]
     my_lanes = pl.ds(pl.multiple_of(x * lanes_x, 128), lanes_x)
 
-    def two_y():
+    def layer_two():
+        wait(rows_hidden)
+        agg = dot(cm[...], t2[...]) * inv[...]
+        joined[:, w:] = agg.astype(BF)
+        both = joined[...]
+        out[0] = dot(both, w_two[...]).astype(BF)
+        two_part = dot(both.T, grads[...]).astype(BF)
+        for f in range(feat):
+            ts[f % 2, (f // 2) * span : (f // 2 + 1) * span] = two_part[f * span : (f + 1) * span]
+        return send(ts.at[1 - c], u1, mate)
+
+    def two_y(two_core):
         two_core.wait_recv()
         ub[...] = (ts[c].astype(F32) + u1[...].astype(F32)).astype(BF)
         return [
@@ -384,16 +389,17 @@
     moves = {}
     marks = [len(copies)]
     drained = 0
-    two_moves = two_y()
     for k in range(half):
         wait(gathers[k])
         moves[k] = chunk(k)
+    two_core = layer_two()
     for k in range(half, chunks):
         gathers[k] = gather_end(k, *gathers[k])
     for k in range(half, chunks):
         wait(gathers[k])
         moves[k] = chunk(k)
         moves[k - half] = z_exchange(k - half, moves[k - half])
+    two_moves = two_y(two_core)
     two_stages = [two_x, two_z, two_zg, two_xg]
     for step in range(1, chunks + 3):
         marks.append(len(copies))
@@ -454,7 +460,7 @@
     lanes_x = w // nx
     chunks = 2 * w // TILE
     n_copies = (
-        3 + 2 * (ny - 1) + 4 * (parts - 1)
+        2 + feat + 2 * (ny - 1) + 4 * (parts - 1)
         + chunks * (4 * ny + 2 + 4 * nx + nz)
         + 2 + 4 * ny + 2 * (nx + nz)
     )

time: 94.6 us -> 94.4 us (level)
  no operation moved by 1% of the time
where the time goes in v6:
time: 94.4 us; the launch traced here: 94.3 us
  Pallas kernels  93.6 us (99%)
    pallas_call x1, Pallas kernels, on_device(): pl.pallas_call(functools.partial(kernel, feat, nx, nz, kmax), out_shape=(...  90.8 us
    pallas_call x1, Pallas kernels, on_device(): pl.pallas_call(functools.partial(finish, scale), out_shape=wide, in_specs...  2.8 us

profile of v6, /device:TPU:0, one launch (start us, length us, event | category | flops | bytes accessed | tf_op | source)
XLA Modules:
  0.0 94.3 jit_solution(3374373888459638341)
XLA Ops:
  0.6 90.8 %shard_map.94 = (bf16[1,128,512]{2,1,0:T(8,128)(2,1)S(1)}, bf16[4,1024,256]{2,1,0:T(8,128)(2,1)S(1)}, bf16[1024,512]{1,0:T(8,128)(2,1)S(1)}) custom-call(bf16[4,128,1024]{2,1,0:T(8,128)(2,1)} %feats_hbm.1, bf16[1024,1024]{1,0:T(8,128)(2,1)} %w_one_hbm.1, bf16[1024,512]{1,0:T(8,128)(2,1)} %w_two_hbm.1, s32[10,1,128]{2,1,0:T(1,128)} %bitcast.4, ...), custom_call_target="tpu_custom_call" | custom-call | tf_op jit(solution)/shard_map/pallas_call | solution.py:490
  91.5 2.8 %shard_map.95 = (bf16[1,128,512]{2,1,0:T(8,128)(2,1)}, f32[1024,1024]{1,0:T(8,128)}, f32[1024,512]{1,0:T(8,128)}) custom-call(bf16[1,128,512]{2,1,0:T(8,128)(2,1)S(1)} %get-tuple-element.6.out, bf16[4,1024,256]{2,1,0:T(8,128)(2,1)S(1)} %get-tuple-element.7.one, bf16[1024,512]{1,0:T(8,128)(2,1)S(1)} %get-tuple-element.8.two), custom_call_target="tpu_custom_call" | custom-call | tf_op jit(solution)/shard_map/pallas_call | solution.py:516

commit v7 on v6

--- a/solution.py
+++ b/solution.py
@@ -27,7 +27,7 @@
     feats_hbm, w_one_hbm, w_two_hbm, nbr_hbm, deg_hbm, sends_hbm, grads_hbm,
     out, one, two,
     feats, w_one, w_two, nbr, deg, sends, grads,
-    proj, projb, r1, q, qb, r2, cm, ct, sm, st, t1, t2, b1, b2, k0, k1, h0, h1,
+    proj, projb, r1, q, qb, r2, cm, ct, cf, cft, sm, st, t1, t2, b1, b2, k0, k1, h0, h1,
     inv, dcs, dh, pself, dnl, joined, fx, ft, dp, g, rx, rz, ts, u1, ub, u2, v, vx, vs, vz,
     ssem, rsem, lsem,
 ):
@@ -119,21 +119,30 @@
     def slot(p):
         return pl.ds(pl.multiple_of(p * SLOT, SLOT), SLOT)
 
-    def table_slot(p):
-        return pl.ds(pl.multiple_of(n + p * SLOT, SLOT), SLOT)
+    wide = w // 2
 
     def trade_rows(values, boxes, table):
-        table[:n] = values
-        boxes[...] = dot(sm[...], values).astype(BF)
-        table[table_slot(di)] = boxes[slot(di)]
-        return [send(boxes.at[slot(p)], table.at[table_slot(di)], (fi, p)) for p in dpeers]
+        boxes[...] = (dot(sm[0], values[:, :wide]) + dot(sm[1], values[:, wide:])).astype(BF)
+        table[slot(di)] = boxes[slot(di)]
+        return [send(boxes.at[slot(p)], table.at[slot(di)], (fi, p)) for p in dpeers]
+
+    def table_mean(values, table):
+        rows = table[...]
+        far = jnp.concatenate([dot(cf[0], rows), dot(cf[1], rows)], axis=1)
+        return (dot(cm[...], values) + far) * inv[...]
 
     def trade_back(values, outgoing, returned):
-        terms = dot(ct[...], (values * inv[...]).astype(BF))
-        outgoing[...] = terms[n:].astype(BF)
+        scaled = (values * inv[...]).astype(BF)
+        outgoing[...] = (
+            dot(cft[0], scaled[:, :wide]) + dot(cft[1], scaled[:, wide:])
+        ).astype(BF)
         returned[slot(di)] = outgoing[slot(di)]
         moves = [send(outgoing.at[slot(p)], returned.at[slot(di)], (fi, p)) for p in dpeers]
-        return terms[:n], moves
+        return dot(ct[...], scaled), moves
+
+    def come_home(returned):
+        rows = returned[...]
+        return jnp.concatenate([dot(st[0], rows), dot(st[1], rows)], axis=1)
 
     def pass_on(low, f, k, device):
         block = dp.at[low, f, k]
@@ -194,43 +203,50 @@
         item.wait()
     eye = lax.broadcasted_iota(jnp.int32, (n, n), 0) == lax.broadcasted_iota(jnp.int32, (n, n), 1)
     inv[...] = 1.0 / jnp.sum(jnp.where(eye, deg[...].astype(F32), 0.0), axis=1, keepdims=True)
-    entry = lax.broadcasted_iota(jnp.int32, (n + parts * SLOT, n), 0)
-    extra = entry - n
-    code = jnp.where(
-        entry < n, entry,
-        jnp.where((extra & 15) < kmax, n + (extra >> 4) * kmax + (extra & 15), -2),
-    )
-    counts = jnp.zeros(code.shape, F32)
-    for s in range(fan):
-        used = jnp.where(s < deg[...], nbr[s], -1)
-        counts = counts + jnp.where(used == code, 1.0, 0.0)
-    ct[...] = counts.astype(BF)
-    cm[...] = counts.T.astype(BF)
+    def tally(code):
+        total = jnp.zeros(code.shape, F32)
+        for s in range(fan):
+            used = jnp.where(s < deg[...], nbr[s], -1)
+            total = total + jnp.where(used == code, 1.0, 0.0)
+        return total
+
+    own = tally(lax.broadcasted_iota(jnp.int32, (n, n), 0))
+    ct[...] = own.astype(BF)
+    cm[...] = own.T.astype(BF)
+    entry = lax.broadcasted_iota(jnp.int32, (parts * SLOT, n), 0)
+    for h in range(2):
+        k = (entry & 15) - h * kmax
+        far = tally(jnp.where((k >= 0) & (k < kmax), n + (entry >> 4) * kmax + k, -2))
+        cft[h] = far.astype(BF)
+        cf[h] = far.T.astype(BF)
     edge = (parts * SLOT, parts)
     owner = lax.broadcasted_iota(jnp.int32, edge, 0) >> 4 == lax.broadcasted_iota(jnp.int32, edge, 1)
     spread_rows = dot(jnp.where(owner, 1.0, 0.0).astype(BF), sends[...].astype(F32).astype(BF))
     place = (parts * SLOT, kmax)
-    here = lax.broadcasted_iota(jnp.int32, place, 0) & 15 == lax.broadcasted_iota(jnp.int32, place, 1)
-    chosen = jnp.sum(jnp.where(here, spread_rows + 1.0, 0.0), axis=1, keepdims=True) - 1.0
+    spot = lax.broadcasted_iota(jnp.int32, place, 0) & 15
     lane = lax.broadcasted_iota(jnp.int32, (parts * SLOT, n), 1).astype(F32)
-    picks = jnp.where(chosen == lane, 1.0, 0.0)
-    sm[...] = picks.astype(BF)
-    st[...] = picks.T.astype(BF)
+    for h in range(2):
+        here = spot == lax.broadcasted_iota(jnp.int32, place, 1) + h * kmax
+        chosen = jnp.sum(jnp.where(here, spread_rows + 1.0, 0.0), axis=1, keepdims=True) - 1.0
+        picks = jnp.where(chosen == lane, 1.0, 0.0)
+        sm[h] = picks.astype(BF)
+        st[h] = picks.T.astype(BF)
     dcat = dot_nt(grads[...], w_two[...])
     dcs[...] = dcat[:, :w]
     local, back_agg = trade_back(dcat[:, w:], k0, h0)
     dcs[...] += local
 
     wait(near_y)
-    rows_near = trade_rows(owned(1).astype(BF), b1, t1)
+    p_near = owned(1).astype(BF)
+    rows_near = trade_rows(p_near, b1, t1)
     features_moves += [send_features(f) for f in range(feat // 2, feat)]
     ft[zlow] = feats[:, :, near_cols].reshape(feat * n, half_cols).T
     wait(self_y)
     pself[...] = owned(0)
     wait(back_agg)
-    dh[...] = dcs[...] + dot(st[...], h0[...])
+    dh[...] = dcs[...] + come_home(h0)
     wait(rows_near)
-    pre = pself[...] + dot(cm[...], t1[...]) * inv[...]
+    pre = pself[...] + table_mean(p_near, t1)
     sig = 1.0 / (1.0 + jnp.exp(-pre))
     d_pre = dh[...] * sig * (1.0 + pre * (1.0 - sig))
     chunks = 2 * w // TILE
@@ -249,7 +265,7 @@
     wait(features_moves)
     ft[1 - zlow] = fx[...].reshape(feat * n, half_cols).T
     wait(back_pre)
-    d_near = (dnl[...] + dot(st[...], h1[...])).astype(BF)
+    d_near = (dnl[...] + come_home(h1)).astype(BF)
     for k in range(half):
         dp[zlow, fi, half + k] = d_near[:, k * TILE : (k + 1) * TILE]
     for k in range(half, chunks):
@@ -319,7 +335,7 @@
 
     def layer_two():
         wait(rows_hidden)
-        agg = dot(cm[...], t2[...]) * inv[...]
+        agg = table_mean(joined[:, :w], t2)
         joined[:, w:] = agg.astype(BF)
         both = joined[...]
         out[0] = dot(both, w_two[...]).astype(BF)
@@ -452,7 +468,6 @@
     w = w_two.shape[1]
     ny = feat // 2
     parts, kmax = send_rows.shape[1:]
-    table = n + parts * SLOT
     edge = parts * SLOT
     half_cols = cols // 2
     rows_x = half_cols // nx
@@ -471,9 +486,11 @@
         vm((parts, kmax), jnp.int32), vm((n, w), BF),
         vm((2, 2, ny * n, w), F32), vm((2, 2, ny * n, w), BF), vm((2, ny * n, w), BF),
         vm((2, n, w), F32), vm((2, ny, n, w), BF), vm((2, ny - 1, n, w), BF),
-        vm((n, table), BF), vm((table, n), BF), vm((edge, n), BF), vm((n, edge), BF),
-        vm((table, w), BF), vm((table, w), BF), vm((edge, w), BF), vm((edge, w), BF),
-        vm((edge, w), BF), vm((edge, w), BF), vm((edge, w), BF), vm((edge, w), BF),
+        vm((n, n), BF), vm((n, n), BF), vm((2, n, edge), BF), vm((2, edge, n), BF),
+        vm((2, edge, n), BF), vm((2, n, edge), BF),
+        vm((edge, w // 2), BF), vm((edge, w // 2), BF), vm((edge, w // 2), BF),
+        vm((edge, w // 2), BF), vm((edge, w // 2), BF), vm((edge, w // 2), BF),
+        vm((edge, w // 2), BF), vm((edge, w // 2), BF),
         vm((n, 1), F32), vm((n, w), F32), vm((n, w), F32), vm((n, w), F32), vm((n, w), F32),
         vm((n, 2 * w), BF), vm((feat, n, half_cols), BF), vm((2, half_cols, feat * n), BF),
         vm((2, feat, chunks, n, TILE), BF),

time: 94.4 us -> 88.5 us (0.937)
  Pallas kernels: 93.6 us -> 87.8 us
    pallas_call x1, Pallas kernels: 90.8 us -> 85 us  [on_device(): pl.pallas_call(functools.partial(kernel, feat, nx, nz, kmax), out_shape=(...]
where the time goes in v7:
time: 88.5 us; the launch traced here: 88.4 us
  Pallas kernels  87.8 us (99%)
    pallas_call x1, Pallas kernels, on_device(): pl.pallas_call(functools.partial(kernel, feat, nx, nz, kmax), out_shape=(...  85 us
    pallas_call x1, Pallas kernels, on_device(): pl.pallas_call(functools.partial(finish, scale), out_shape=wide, in_specs...  2.8 us

profile of v7, /device:TPU:0, one launch (start us, length us, event | category | flops | bytes accessed | tf_op | source)
XLA Modules:
  0.0 88.4 jit_solution(11387599009977923615)
XLA Ops:
  0.6 85.0 %shard_map.94 = (bf16[1,128,512]{2,1,0:T(8,128)(2,1)S(1)}, bf16[4,1024,256]{2,1,0:T(8,128)(2,1)S(1)}, bf16[1024,512]{1,0:T(8,128)(2,1)S(1)}) custom-call(bf16[4,128,1024]{2,1,0:T(8,128)(2,1)} %feats_hbm.1, bf16[1024,1024]{1,0:T(8,128)(2,1)} %w_one_hbm.1, bf16[1024,512]{1,0:T(8,128)(2,1)} %w_two_hbm.1, s32[10,1,128]{2,1,0:T(1,128)} %bitcast.4, ...), custom_call_target="tpu_custom_call" | custom-call | tf_op jit(solution)/shard_map/pallas_call | solution.py:507
  85.6 2.8 %shard_map.95 = (bf16[1,128,512]{2,1,0:T(8,128)(2,1)}, f32[1024,1024]{1,0:T(8,128)}, f32[1024,512]{1,0:T(8,128)}) custom-call(bf16[1,128,512]{2,1,0:T(8,128)(2,1)S(1)} %get-tuple-element.6.out, bf16[4,1024,256]{2,1,0:T(8,128)(2,1)S(1)} %get-tuple-element.7.one, bf16[1024,512]{1,0:T(8,128)(2,1)S(1)} %get-tuple-element.8.two), custom_call_target="tpu_custom_call" | custom-call | tf_op jit(solution)/shard_map/pallas_call | solution.py:533

commit v8 on v7

--- a/solution.py
+++ b/solution.py
@@ -11,7 +11,8 @@
 BF = jnp.bfloat16
 F32 = jnp.float32
 SLOT = 16
-TILE = 256
+TILE = 128
+BROAD = 256
 
 
 def dot(a, b):
@@ -83,12 +84,12 @@
 
     def project(h):
         flat = feats[...].reshape(feat * n, cols)
-        for t in range(w // TILE):
-            acc = dot(flat, w_one[:, h * w + t * TILE : h * w + (t + 1) * TILE])
+        for t in range(w // BROAD):
+            acc = dot(flat, w_one[:, h * w + t * BROAD : h * w + (t + 1) * BROAD])
             for f in range(feat):
                 part = acc[f * n : (f + 1) * n]
                 rows = slice((f // 2) * n, (f // 2 + 1) * n)
-                lanes = slice(t * TILE, (t + 1) * TILE)
+                lanes = slice(t * BROAD, (t + 1) * BROAD)
                 proj[h, f % 2, rows, lanes] = part
                 projb[h, f % 2, rows, lanes] = part.astype(BF)
 

time: 88.5 us -> 91.8 us (1.037)
  Pallas kernels: 87.8 us -> 91.1 us
    pallas_call x1, Pallas kernels: 85 us -> 88.2 us  [on_device(): pl.pallas_call(functools.partial(kernel, feat, nx, nz, kmax), out_shape=(...]
where the time goes in v8:
time: 91.8 us; the launch traced here: 91.7 us
  Pallas kernels  91.1 us (99%)
    pallas_call x1, Pallas kernels, on_device(): pl.pallas_call(functools.partial(kernel, feat, nx, nz, kmax), out_shape=(...  88.2 us
    pallas_call x1, Pallas kernels, on_device(): pl.pallas_call(functools.partial(finish, scale), out_shape=wide, in_specs...  2.85 us

profile of v8, /device:TPU:0, one launch (start us, length us, event | category | flops | bytes accessed | tf_op | source)
XLA Modules:
  0.0 91.7 jit_solution(17093415191192734255)
XLA Ops:
  0.6 88.2 %shard_map.94 = (bf16[1,128,512]{2,1,0:T(8,128)(2,1)S(1)}, bf16[8,1024,128]{2,1,0:T(8,128)(2,1)S(1)}, bf16[1024,512]{1,0:T(8,128)(2,1)S(1)}) custom-call(bf16[4,128,1024]{2,1,0:T(8,128)(2,1)} %feats_hbm.1, bf16[1024,1024]{1,0:T(8,128)(2,1)} %w_one_hbm.1, bf16[1024,512]{1,0:T(8,128)(2,1)} %w_two_hbm.1, s32[10,1,128]{2,1,0:T(1,128)} %bitcast.4, ...), custom_call_target="tpu_custom_call" | custom-call | tf_op jit(solution)/shard_map/pallas_call | solution.py:508
  88.8 2.9 %shard_map.95 = (bf16[1,128,512]{2,1,0:T(8,128)(2,1)}, f32[1024,1024]{1,0:T(8,128)}, f32[1024,512]{1,0:T(8,128)}) custom-call(bf16[1,128,512]{2,1,0:T(8,128)(2,1)S(1)} %get-tuple-element.6.out, bf16[8,1024,128]{2,1,0:T(8,128)(2,1)S(1)} %get-tuple-element.7.one, bf16[1024,512]{1,0:T(8,128)(2,1)S(1)} %get-tuple-element.8.two), custom_call_target="tpu_custom_call" | custom-call | tf_op jit(solution)/shard_map/pallas_call | solution.py:534
